TPU v7x, 512 devices: a whole 4x4x16 slice. The times are simulated.
512 devices in a mesh: dp: 8 (over z_hi, core), state: 64 (over y, x, z_lo).
Axes of the slice: x: 4, y: 4, z: 16 (z_hi: 4, z_lo: 4; z = z_hi * 4 + z_lo), core: 2. Of those that a mesh axis runs over, the one named last changes fastest.
Arguments:
- forward_probs: float32 [2, 512, 8192], P(None, 'dp', 'state'), as said below
- backward_last: float32 [512, 8192], P('dp', 'state'), as said below
- emission: float32 [1024, 8192], P(None, 'state'), as said below
- token_ids: int32 [512, 2], P('dp'), may hold values from 0 to 1023
- transition: bfloat16 [8192, 8192], P('state'), as said below
Outputs:
- backward_first: float32 [512, 8192], P('dp', 'state')
- count_ratio: float32 [8192, 8192], P('state', 'dp')
Inputs may be any that keep to these rules, and one draw needn't show every extreme that they name: `transition`: positive weights. `emission`: positive. `forward_probs`: positive. `backward_last`: positive.
All inputs are finite; a program needn't handle non-finite values.
Results may differ from a plain program's by a relative error of at most 0.0029.
Values may be sent and summed in bfloat16 or wider, within the bound.
No kernel may reach another device: no remote copies, remote signals or barrier semaphores. Data moves between devices by JAX's collectives and lax.ppermute only.
A program may use at most 64 MiB of HBM per device.

v0:
```python
import jax
import jax.numpy as jnp
from jax import lax
from jax.sharding import PartitionSpec as P


def on_device(forward_probs, backward_last, emission, token_ids, transition):
    width = transition.shape[1]
    seq_total = backward_last.shape[0] * lax.axis_size("dp")
    backward = backward_last
    accum = None
    for step in reversed(range(forward_probs.shape[0])):
        emitted = jnp.take(emission, token_ids[:, step], axis=0)
        weighted = (emitted * backward).astype(jnp.bfloat16)
        gathered = lax.all_gather(weighted, "state", axis=1, tiled=True)
        propagated = lax.dot_general(
            gathered, transition, (((1,), (1,)), ((), ())), preferred_element_type=jnp.float32
        )
        totals = lax.psum(
            (jnp.sum(propagated, axis=1), jnp.sum(forward_probs[step] * propagated, axis=1)),
            "state",
        )
        scale_back = totals[0] / width
        scale_post = totals[1] / width
        backward = propagated / scale_back[:, None]
        posterior = (forward_probs[step] / scale_post[:, None]).astype(jnp.bfloat16)
        rows_all = lax.all_gather(posterior, "dp", axis=0, tiled=True)
        columns = lax.all_to_all(gathered, "dp", split_axis=1, concat_axis=0, tiled=True)
        term = lax.dot_general(
            rows_all, columns, (((0,), (0,)), ((), ())), preferred_element_type=jnp.float32
        )
        accum = term if accum is None else accum + term
    return (backward, accum / (forward_probs.shape[0] * seq_total))


def solution(mesh):
    placed = (
        P(None, "dp", "state"),
        P("dp", "state"),
        P(None, "state"),
        P("dp", None),
        P("state", None),
    )
    return jax.shard_map(
        on_device,
        mesh=mesh,
        in_specs=placed,
        out_specs=(P("dp", "state"), P("state", "dp")),
        check_vma=False,
    )
```

profile of v0, /device:TPU:1, one launch (start us, length us, event | category | flops | bytes accessed | tf_op | source)
XLA Modules:
  0.0 1085.9 jit_solution(1363672242504539797)
XLA Ops:
  7.2 0.0 copy-start
  7.2 0.0 all-gather.3.cloned.1.call-start
  7.2 0.8 compare_and_fusion
  8.1 1.6 gather_fusion.1
  9.7 1.4 fusion.5
  11.2 0.0 all-gather.3.cloned.1.call-update
  11.2 245.4 %all-gather.3.cloned.1.call-done = bf16[64,8192]{1,0:T(8,128)(2,1)} async-done(((bf16[64,128]{1,0:T(8,128)(2,1)}), bf16[64,8192]{1,0:T(8,128)(2,1)}) %all-gather.3.cloned.1.call-update) | async-done | bytes 1048592 | tf_op jit(solution)/shard_map/all_gather | solution.py:15
  256.6 0.0 copy-start.1
  256.6 2.4 copy.14
  259.0 44.9 %all-to-all-start = ((bf16[64,8,1024]{2,0,1:T(8,128)(2,1)}), bf16[64,8,1024]{2,0,1:T(8,128)(2,1)}, u32[]{:S(2)}, u32[]{:S(2)}) async-start(bf16[64,8,1024]{2,0,1:T(8,128)(2,1)} %bitcast.41), calls=%async_computation | async-start | bytes 2097152 | tf_op jit(solution)/shard_map/all_to_all | solution.py:28
  303.9 0.0 all-gather.5.cloned.1.call-start
  303.9 1.6 gather_fusion
  305.5 0.0 copy-done
  305.5 0.0 copy-done.1
  305.5 0.9 fusion.7
  306.5 191.0 %psum.28 = f32[64]{0:T(128)S(1)} all-reduce(f32[64]{0:T(128)S(1)} %get-tuple-element.17), channel_id=1, replica_groups=mesh['dp'=8,'state'=64] {'state'}, use_global_device_ids=true, to_apply=%region_1.3 | all-reduce | flops 64 | bytes 512 | tf_op jit(solution)/shard_map/psum | solution.py:19
  497.5 0.7 fusion.6
  498.2 0.0 all-gather.5.cloned.1.call-update
  498.2 264.3 %all-gather.5.cloned.1.call-done = bf16[64,8192]{1,0:T(8,128)(2,1)} async-done(((bf16[64,128]{1,0:T(8,128)(2,1)}), bf16[64,8192]{1,0:T(8,128)(2,1)}) %all-gather.5.cloned.1.call-update) | async-done | bytes 1048592 | tf_op jit(solution)/shard_map/all_gather | solution.py:15
  762.6 2.3 copy.13
  764.9 0.0 all-to-all-done
  764.9 44.9 %all-to-all-start.1 = ((bf16[64,8,1024]{2,0,1:T(8,128)(2,1)}), bf16[64,8,1024]{2,0,1:T(8,128)(2,1)S(1)}, u32[]{:S(2)}, u32[]{:S(2)}) async-start(bf16[64,8,1024]{2,0,1:T(8,128)(2,1)} %bitcast.40), calls=%async_computation.1 | async-start | bytes 2097152 | tf_op jit(solution)/shard_map/all_to_all | solution.py:28
  809.8 0.0 copy-done.2
  809.8 2.2 fusion.1
  812.0 191.5 %all-reduce = (f32[64]{0:T(128)S(1)}, f32[64]{0:T(128)S(1)}, f32[64]{0:T(128)S(1)}) all-reduce(f32[64]{0:T(128)S(1)} %get-tuple-element.5, f32[64]{0:T(128)S(1)} %get-tuple-element.4, f32[64]{0:T(128)S(1)} %get-tuple-element.3), channel_id=1, replica_groups=mesh['dp'=8,'state'=64] {'state'}, use_global_device_ids=true, to_apply=%region_3.5 | all-reduce | flops 192 | bytes 1536 | tf_op jit(solution)/shard_map/psum | solution.py:19
  1003.5 0.1 fusion.2
  1003.6 52.0 %all_gather.14 = bf16[512,128]{1,0:T(8,128)(2,1)S(1)} all-gather(bf16[64,128]{1,0:T(8,128)(2,1)S(1)} %get-tuple-element.14), channel_id=1, replica_groups=mesh['dp'=8,'state'=64] {'dp'}, dimensions={0}, use_global_device_ids=true | all-gather | bytes 147456 | tf_op jit(solution)/shard_map/all_gather | solution.py:27
  1055.6 18.2 %all_gather.15 = bf16[512,128]{1,0:T(8,128)(2,1)S(1)} all-gather(bf16[64,128]{1,0:T(8,128)(2,1)S(1)} %get-tuple-element.13), channel_id=1, replica_groups=mesh['dp'=8,'state'=64] {'dp'}, dimensions={0}, use_global_device_ids=true | all-gather | bytes 147456 | tf_op jit(solution)/shard_map/all_gather | solution.py:27
  1073.8 0.7 broadcast_divide_fusion
  1074.5 2.4 fusion.8
  1076.9 0.0 all-to-all-done.1
  1076.9 2.2 fusion
  (6 shorter events, 0.0 us)
Async XLA Ops:
  7.2 298.4 %copy-start = (bf16[128,8192]{1,0:T(8,128)(2,1)S(1)}, bf16[128,8192]{1,0:T(8,128)(2,1)}, u32[]{:S(2)}) copy-start(bf16[128,8192]{1,0:T(8,128)(2,1)} %param.11) | copy-start | bytes 6291460
  7.2 249.4 %all-gather.3.cloned.1.call-start = ((), (), s32[]{:S(2)}) async-start(), calls=%async_computation.2 | async-start | bytes 1064960 | tf_op jit(solution)/shard_map/all_gather | solution.py:15
  256.6 49.0 %copy-start.1 = (bf16[64,8192]{1,0:T(8,128)(2,1)S(1)}, bf16[64,8192]{1,0:T(8,128)(2,1)}, u32[]{:S(2)}) copy-start(bf16[64,8192]{1,0:T(8,128)(2,1)} %all-gather.3.cloned.1.call-done) | copy-start | bytes 3145732
  259.0 505.9 %all-to-all-start = ((bf16[64,8,1024]{2,0,1:T(8,128)(2,1)}), bf16[64,8,1024]{2,0,1:T(8,128)(2,1)}, u32[]{:S(2)}, u32[]{:S(2)}) async-start(bf16[64,8,1024]{2,0,1:T(8,128)(2,1)} %bitcast.41), calls=%async_computation | async-start | bytes 2097152 | tf_op jit(solution)/shard_map/all_to_all | solution.py:28
  303.9 458.7 %all-gather.5.cloned.1.call-start = ((), (), s32[]{:S(2)}) async-start(), calls=%async_computation.3 | async-start | bytes 1064960 | tf_op jit(solution)/shard_map/all_gather | solution.py:15
  762.6 47.2 %copy-start.2 = (f32[2,64,128]{2,1,0:T(8,128)S(1)}, f32[2,64,128]{2,1,0:T(8,128)}, u32[]{:S(2)}) copy-start(f32[2,64,128]{2,1,0:T(8,128)} %param.7) | copy-start | bytes 196612
  764.9 311.9 %all-to-all-start.1 = ((bf16[64,8,1024]{2,0,1:T(8,128)(2,1)}), bf16[64,8,1024]{2,0,1:T(8,128)(2,1)S(1)}, u32[]{:S(2)}, u32[]{:S(2)}) async-start(bf16[64,8,1024]{2,0,1:T(8,128)(2,1)} %bitcast.40), calls=%async_computation.1 | async-start | bytes 2097152 | tf_op jit(solution)/shard_map/all_to_all | solution.py:28
Sparse Core Ops, SparseCore 0:
  11.3 245.2 all-gather.2
  498.4 264.1 all-gather.4
where the time goes:
time: 1090 us
  waiting for transfers between devices  510 us (47%)
  blocking collectives  453 us (42%)
  starting transfers between devices  89.8 us (8%)
  between operations  14.1 us (1%)
    all_gather x2, waiting for transfers between devices, on_device(): gathered = lax.all_gather(weighted, 'state', axis=1, tiled=True)  510 us
    psum x2, blocking collectives, on_device(): lax.psum((jnp.sum(propagated, axis=1), jnp.sum(forward_probs[step] * prop...  383 us
    all_to_all x2, starting transfers between devices, on_device(): lax.all_to_all(gathered, 'dp', split_axis=1, concat_axis=0, tiled=True)  89.8 us
    all_gather x2, blocking collectives, on_device(): rows_all = lax.all_gather(posterior, 'dp', axis=0, tiled=True)  70.2 us
  transfers between devices with their start and end apart: 4, of which 2 were waited for; matrix products, arithmetic and copies ran while one was open for 1% of the time, Pallas kernels for 0%

commit v1 on v0

v1 whole, which is shorter than its diff:
```python
import jax
import jax.numpy as jnp
from jax import lax
from jax.sharding import Mesh, PartitionSpec as P

SIZES = (4, 2, 4, 2, 2, 4)
AXES = ("zh", "co", "y", "xh", "xl", "zl")
DP = ("zh", "co")
STATE = ("y", "xh", "xl", "zl")
PLANE = ("y", "xh", "xl")
LINE = ("zh", "co", "zl")


def spread(block, axes):
    count = lax.axis_size(axes)
    return lax.all_to_all(
        jnp.broadcast_to(block[None], (count,) + block.shape), axes, 0, 0, tiled=True
    )


def split3(value):
    high = lax.reduce_precision(value, 8, 7)
    middle = lax.reduce_precision(value - high, 8, 7)
    low = value - high - middle
    return jnp.stack([high, middle, low]).astype(jnp.bfloat16)


def swap_groups(block):
    pairs = []
    for source in range(512):
        zl, xl, xh = source % 4, source // 4 % 2, source // 8 % 2
        y, co, zh = source // 16 % 4, source // 64 % 2, source // 128
        pairs.append((source, ((((y * 2 + xh) * 4 + zh) * 2 + co) * 2 + xl) * 4 + zl))
    return lax.ppermute(block, AXES, pairs)


def on_device(forward_probs, backward_last, emission, token_ids, transition):
    rows, width = transition.shape
    seqs = backward_last.shape[0]
    steps = forward_probs.shape[0]
    groups = lax.axis_size(DP)

    forward_all = lax.all_gather(forward_probs, DP)
    emitted = jnp.take(emission, token_ids.T.reshape(-1), axis=0).reshape(steps, seqs, rows)

    weighted = (emitted[1] * backward_last).astype(jnp.bfloat16)
    col_sums = split3(jnp.sum(transition.astype(jnp.float32), axis=0).reshape(-1, rows))
    packed = spread(jnp.concatenate([weighted[None], col_sums]), "zl")
    line1 = packed[:, 0]
    col_line = split3(jnp.sum(packed[:, 1:].astype(jnp.float32), axis=(0, 1)))
    far1 = swap_groups(line1)
    packed = spread(jnp.concatenate([line1, col_line]), PLANE)
    gathered = packed[:, :4].reshape(-1, seqs, rows)
    col_all = jnp.sum(packed[:, 4:].astype(jnp.float32), axis=(0, 1))
    columns1 = lax.all_gather(far1, PLANE)

    trans = transition.reshape(rows, -1, rows)
    prop1 = lax.dot_general(
        gathered, trans, (((0, 2), (1, 2)), ((), ())), preferred_element_type=jnp.float32
    )
    norm = jnp.sum(gathered.astype(jnp.float32) * col_all[:, None, :], axis=(0, 2)) / width
    post1 = jnp.sum(forward_probs[1] * prop1, axis=1)
    weighted = (emitted[0] * (prop1 / norm[:, None])).astype(jnp.bfloat16)

    line0 = spread(weighted, "zl")
    far0 = swap_groups(line0)
    gathered = spread(line0, PLANE).reshape(-1, seqs, rows)
    prop0 = lax.dot_general(
        gathered, trans, (((0, 2), (1, 2)), ((), ())), preferred_element_type=jnp.float32
    )
    sums = jnp.stack([post1, jnp.sum(forward_probs[0] * prop0, axis=1), jnp.sum(prop0, axis=1)])
    columns0 = spread(far0, PLANE)
    sums = jnp.sum(spread(sums, PLANE), axis=0)
    sums = jnp.sum(spread(sums, LINE).reshape(groups, -1, 3, seqs), axis=1) / width
    mine = lax.dynamic_index_in_dim(sums, lax.axis_index(DP), 0, keepdims=False)
    backward = prop0 / mine[2][:, None]
    total = None
    for step, columns, post in ((1, columns1, sums[:, 0]), (0, columns0, sums[:, 1])):
        posterior = (forward_all[:, step] / post[:, :, None]).astype(jnp.bfloat16)
        cols = columns.reshape(groups, -1, seqs, rows)
        term = lax.dot_general(
            posterior, cols, (((0, 1), (0, 2)), ((), ())), preferred_element_type=jnp.float32
        )
        total = term if total is None else total + term
    return (backward, total.reshape(rows, -1) / (steps * groups * seqs))


def solution(mesh):
    fine = Mesh(mesh.devices.reshape(SIZES), AXES)
    placed = (P(None, DP, STATE), P(DP, STATE), P(None, STATE), P(DP, None), P(STATE, None))
    return jax.shard_map(
        on_device,
        mesh=fine,
        in_specs=placed,
        out_specs=(P(DP, STATE), P(STATE, DP)),
        check_vma=False,
    )
```

time: 1090 us -> 192 us (0.18)
  waiting for transfers between devices: 510 us -> 16.8 us
  blocking collectives: 453 us -> 97.5 us
  starting transfers between devices: 89.8 us -> 43.3 us
    all_gather x2 -> x1, waiting for transfers between devices: 510 us -> 0.02 us  [on_device(): columns1 = lax.all_gather(far1, PLANE)]
    psum x2 -> x0, blocking collectives: 383 us -> none  [on_device(): lax.psum((jnp.sum(propagated, axis=1), jnp.sum(forward_probs[step] * prop...]
    all_to_all x0 -> x4, blocking collectives: none -> 68.1 us  [spread(): lax.all_to_all(jnp.broadcast_to(block[None], (count,) + block.shape), axe...]
    all_to_all x2 -> x3, starting transfers between devices: 89.8 us -> 31.5 us  [spread(): lax.all_to_all(jnp.broadcast_to(block[None], (count,) + block.shape), axe...]
    all_gather x2 -> x1, blocking collectives: 70.2 us -> 29.3 us  [on_device(): forward_all = lax.all_gather(forward_probs, DP)]
    ppermute x0 -> x2, waiting for transfers between devices: none -> 12.1 us  [swap_groups(): return lax.ppermute(block, AXES, pairs)]
    ppermute x0 -> x2, starting transfers between devices: none -> 11.7 us  [swap_groups(): return lax.ppermute(block, AXES, pairs)]
  transfers between devices with their start and end apart: 4 -> 6, of which waited for: 2 -> 3; matrix products, arithmetic and copies ran while one was open for 1% -> 4% of each run, Pallas kernels for 0% -> 0%
where the time goes in v1:
time: 192 us
  blocking collectives  97.5 us (51%)
  starting transfers between devices  43.3 us (23%)
  waiting for transfers between devices  16.8 us (9%)
  between operations  14.3 us (7%)
  local copies, waits for them, and re-layouts  9.51 us (5%)
  matrix products  5.61 us (3%)
  other arithmetic  4.72 us (2%)
    all_to_all x4, blocking collectives, spread(): lax.all_to_all(jnp.broadcast_to(block[None], (count,) + block.shape), axe...  68.1 us
    all_to_all x3, starting transfers between devices, spread(): lax.all_to_all(jnp.broadcast_to(block[None], (count,) + block.shape), axe...  31.5 us
    all_gather x1, blocking collectives, on_device(): forward_all = lax.all_gather(forward_probs, DP)  29.3 us
    ppermute x2, waiting for transfers between devices, swap_groups(): return lax.ppermute(block, AXES, pairs)  12.1 us
    ppermute x2, starting transfers between devices, swap_groups(): return lax.ppermute(block, AXES, pairs)  11.7 us
    all_to_all x3, waiting for transfers between devices, spread(): lax.all_to_all(jnp.broadcast_to(block[None], (count,) + block.shape), axe...  4.74 us
  transfers between devices with their start and end apart: 6, of which 3 were waited for; matrix products, arithmetic and copies ran while one was open for 4% of the time, Pallas kernels for 0%

profile of v1, /device:TPU:1, one launch (start us, length us, event | category | flops | bytes accessed | tf_op | source)
XLA Modules:
  0.0 191.8 jit_solution(7973241787837096365)
XLA Ops:
  7.2 0.8 reshape.153
  8.0 0.8 reshape.152
  8.8 1.9 %convert_reduce_fusion = f32[8192]{0:T(1024)S(1)} fusion(bf16[128,8192]{1,0:T(8,128)(2,1)} %param.9), kind=kLoop, calls=%fused_computation.1 | loop fusion | flops 2088960 | bytes 2129920 | tf_op jit(solution)/shard_map/reduce_sum | solution.py:47
  10.8 0.6 gather_fusion
  11.6 12.2 %all_to_all.35 = bf16[4,4,64,128]{3,2,1,0:T(8,128)(2,1)S(1)} all-to-all(bf16[4,4,64,128]{3,2,1,0:T(8,128)(2,1)S(1)} %broadcast_in_dim.29), channel_id=1, replica_groups=mesh['zh'=4,'co'=2,'y'=4,'xh'=2,'xl'=2,'zl'=4] {'zl'}, dimensions={0} | all-to-all | bytes 524288 | tf_op jit(solution)/shard_map/all_to_all | solution.py:16
  23.9 0.4 broadcast_in_dim.30
  24.4 30.0 %all_to_all.36 = bf16[16,7,64,128]{3,2,1,0:T(8,128)(2,1)S(1)} all-to-all(bf16[16,7,64,128]{3,2,1,0:T(8,128)(2,1)S(1)} %broadcast_in_dim.30), channel_id=1, replica_groups=mesh['zh'=4,'co'=2,'y'=4,'xh'=2,'xl'=2,'zl'=4] {'y','xh','xl'}, dimensions={0} | all-to-all | bytes 3670016 | tf_op jit(solution)/shard_map/all_to_all | solution.py:16
  55.0 1.0 copy-done.1
  56.0 0.8 fusion.26
  56.9 10.1 %all_to_all.37 = bf16[4,64,128]{2,1,0:T(8,128)(2,1)S(1)} all-to-all(bf16[4,64,128]{2,1,0:T(8,128)(2,1)S(1)} %broadcast_in_dim.31), channel_id=1, replica_groups=mesh['zh'=4,'co'=2,'y'=4,'xh'=2,'xl'=2,'zl'=4] {'zl'}, dimensions={0} | all-to-all | bytes 131072 | tf_op jit(solution)/shard_map/all_to_all | solution.py:16
  66.9 1.2 broadcast_in_dim.32
  68.2 4.3 %all-to-all-start.3 = ((bf16[16,4,64,128]{3,2,1,0:T(8,128)(2,1)}), bf16[16,4,64,128]{3,2,1,0:T(8,128)(2,1)}, u32[]{:S(2)}, u32[]{:S(2)}) async-start(bf16[16,4,64,128]{3,2,1,0:T(8,128)(2,1)} %broadcast_in_dim.32), calls=%async_computation.3 | async-start | bytes 2097152 | tf_op jit(solution)/shard_map/all_to_all | solution.py:16
  72.6 8.7 %collective-permute-start = (bf16[4,64,128]{2,1,0:T(8,128)(2,1)S(1)}, bf16[4,64,128]{2,1,0:T(8,128)(2,1)S(1)}, u32[]{:S(2)}, u32[]{:S(2)}) collective-permute-start(bf16[4,64,128]{2,1,0:T(8,128)(2,1)S(1)} %slice_bitcast_fusion.2), channel_id=1, source_target_pairs={{0,0},{1,1},{2,2},{3,3},{4,4},{5,5},{6,6},{7,7},{8,64},{9,65},{10,... | collective-permute-start | bytes 196616 | tf_op jit(solution)/shard_map/ppermute | solution.py:34
  81.3 7.7 %collective-permute-done = bf16[4,64,128]{2,1,0:T(8,128)(2,1)S(1)} collective-permute-done((bf16[4,64,128]{2,1,0:T(8,128)(2,1)S(1)}, bf16[4,64,128]{2,1,0:T(8,128)(2,1)S(1)}, u32[]{:S(2)}, u32[]{:S(2)}) %collective-permute-start) | collective-permute-done | bytes 65568 | tf_op jit(solution)/shard_map/ppermute | solution.py:34
  89.0 0.6 copy-done.3
  89.6 2.2 %fusion.28 = (f32[64]{0:T(128)S(1)}, f32[64]{0:T(128)S(1)}, f32[64]{0:T(128)S(1)}, f32[64,128]{1,0:T(8,128)S(1)}) fusion(f32[64,128]{1,0:T(8,128)S(1)} %get-tuple-element.26, f32[2,64,128]{2,1,0:T(8,128)S(1)} %copy-done.2, bf16[64,64,128]{2,1,0:T(8,128)(2,1)} %bitcast.13, bf16[128,8192]{1,0:T(8,128)(2,1)S(1)} %copy-done.1), kind=kOutput, calls=%fused_computation.47 | convolution fusion | flops 134258496 | bytes 3277568 | tf_op jit(solution)/shard_map/dot_general | solution.py:68
  92.0 15.8 %all_to_all.38 = f32[16,1,192]{2,1,0:T(1,128)S(1)} all-to-all(f32[16,1,192]{2,1,0:T(1,128)S(1)} %reshape.178), channel_id=1, replica_groups=mesh['zh'=4,'co'=2,'y'=4,'xh'=2,'xl'=2,'zl'=4] {'y','xh','xl'}, dimensions={0} | all-to-all | bytes 24576 | tf_op jit(solution)/shard_map/all_to_all | solution.py:16
  107.8 0.5 broadcast.47
  108.3 0.7 reduce.1
  109.1 0.7 reshape.180
  109.8 17.8 %all-to-all-start.5 = ((f32[32,1,192]{2,1,0:T(1,128)}), f32[32,1,192]{2,1,0:T(1,128)S(1)}, u32[]{:S(2)}, u32[]{:S(2)}) async-start(f32[32,1,192]{2,1,0:T(1,128)} %reshape.180), calls=%async_computation.5 | async-start | bytes 65536 | tf_op jit(solution)/shard_map/all_to_all | solution.py:16
  127.6 3.0 %collective-permute-start.1 = (bf16[4,64,128]{2,1,0:T(8,128)(2,1)S(1)}, bf16[4,64,128]{2,1,0:T(8,128)(2,1)S(1)}, u32[]{:S(2)}, u32[]{:S(2)}) collective-permute-start(bf16[4,64,128]{2,1,0:T(8,128)(2,1)S(1)} %all_to_all.37), channel_id=1, source_target_pairs={{0,0},{1,1},{2,2},{3,3},{4,4},{5,5},{6,6},{7,7},{8,64},{9,65},{10,... | collective-permute-start | bytes 196616 | tf_op jit(solution)/shard_map/ppermute | solution.py:34
  130.6 4.4 %collective-permute-done.1 = bf16[4,64,128]{2,1,0:T(8,128)(2,1)S(1)} collective-permute-done((bf16[4,64,128]{2,1,0:T(8,128)(2,1)S(1)}, bf16[4,64,128]{2,1,0:T(8,128)(2,1)S(1)}, u32[]{:S(2)}, u32[]{:S(2)}) %collective-permute-start.1) | collective-permute-done | bytes 65568 | tf_op jit(solution)/shard_map/ppermute | solution.py:34
  135.0 4.7 %all-to-all-done.5 = f32[32,1,192]{2,1,0:T(1,128)S(1)} async-done(((f32[32,1,192]{2,1,0:T(1,128)}), f32[32,1,192]{2,1,0:T(1,128)S(1)}, u32[]{:S(2)}, u32[]{:S(2)}) %all-to-all-start.5) | async-done | bytes 24608 | tf_op jit(solution)/shard_map/all_to_all | solution.py:16
  139.7 1.3 broadcast_in_dim.35
  141.0 9.4 %all-to-all-start.6 = ((bf16[16,4,64,128]{3,2,1,0:T(8,128)(2,1)}), bf16[16,4,64,128]{3,2,1,0:T(8,128)(2,1)S(1)}, u32[]{:S(2)}, u32[]{:S(2)}) async-start(bf16[16,4,64,128]{3,2,1,0:T(8,128)(2,1)} %broadcast_in_dim.35), calls=%async_computation.6 | async-start | bytes 2097152 | tf_op jit(solution)/shard_map/all_to_all | solution.py:16
  150.4 29.3 %all-gather = f32[16,64,128]{2,1,0:T(8,128)S(1)} all-gather(f32[2,64,128]{2,1,0:T(8,128)S(1)} %copy-done.2), channel_id=2, replica_groups=mesh['zh'=4,'co'=2,'y'=4,'xh'=2,'xl'=2,'zl'=4] {'zh','co'}, dimensions={0}, use_global_device_ids=true | all-gather | bytes 589824 | tf_op jit(solution)/shard_map/all_gather | solution.py:43
  179.8 0.7 reduce.2
  180.6 0.7 convolution_bitcast_fusion
  181.3 1.9 fusion.7
  183.2 1.0 copy.50
  184.2 0.7 broadcast_divide_fusion
  (41 shorter events, 1.3 us)
Async XLA Ops:
  7.2 3.6 %copy-start = (f32[1024,128]{1,0:T(8,128)S(1)}, f32[1024,128]{1,0:T(8,128)}, u32[]{:S(2)}) copy-start(f32[1024,128]{1,0:T(8,128)} %param.7) | copy-start | bytes 1572868
  7.2 4.3 %copy-start.4 = (f32[64,128]{1,0:T(8,128)S(1)}, f32[64,128]{1,0:T(8,128)}, u32[]{:S(2)}) copy-start(f32[64,128]{1,0:T(8,128)} %param.6) | copy-start | bytes 98308
  54.4 1.6 copy-start.1
  56.8 32.8 %copy-start.2 = (f32[2,64,128]{2,1,0:T(8,128)S(1)}, f32[2,64,128]{2,1,0:T(8,128)}, u32[]{:S(2)}) copy-start(f32[2,64,128]{2,1,0:T(8,128)} %param.5) | copy-start | bytes 196612
  68.2 21.4 %all-to-all-start.3 = ((bf16[16,4,64,128]{3,2,1,0:T(8,128)(2,1)}), bf16[16,4,64,128]{3,2,1,0:T(8,128)(2,1)}, u32[]{:S(2)}, u32[]{:S(2)}) async-start(bf16[16,4,64,128]{3,2,1,0:T(8,128)(2,1)} %broadcast_in_dim.32), calls=%async_computation.3 | async-start | bytes 2097152 | tf_op jit(solution)/shard_map/all_to_all | solution.py:16
  72.5 108.8 %all-gather.4.cloned.1.call-start = ((), (), s32[]{:S(2)}) async-start(), calls=%async_computation.7 | async-start | bytes 1114112 | tf_op jit(solution)/shard_map/all_gather | solution.py:55
  72.6 16.4 %collective-permute-start = (bf16[4,64,128]{2,1,0:T(8,128)(2,1)S(1)}, bf16[4,64,128]{2,1,0:T(8,128)(2,1)S(1)}, u32[]{:S(2)}, u32[]{:S(2)}) collective-permute-start(bf16[4,64,128]{2,1,0:T(8,128)(2,1)S(1)} %slice_bitcast_fusion.2), channel_id=1, source_target_pairs={{0,0},{1,1},{2,2},{3,3},{4,4},{5,5},{6,6},{7,7},{8,64},{9,65},{10,... | collective-permute-start | bytes 196616 | tf_op jit(solution)/shard_map/ppermute | solution.py:34
  89.0 0.6 copy-start.3
  109.8 29.9 %all-to-all-start.5 = ((f32[32,1,192]{2,1,0:T(1,128)}), f32[32,1,192]{2,1,0:T(1,128)S(1)}, u32[]{:S(2)}, u32[]{:S(2)}) async-start(f32[32,1,192]{2,1,0:T(1,128)} %reshape.180), calls=%async_computation.5 | async-start | bytes 65536 | tf_op jit(solution)/shard_map/all_to_all | solution.py:16
  127.6 7.4 %collective-permute-start.1 = (bf16[4,64,128]{2,1,0:T(8,128)(2,1)S(1)}, bf16[4,64,128]{2,1,0:T(8,128)(2,1)S(1)}, u32[]{:S(2)}, u32[]{:S(2)}) collective-permute-start(bf16[4,64,128]{2,1,0:T(8,128)(2,1)S(1)} %all_to_all.37), channel_id=1, source_target_pairs={{0,0},{1,1},{2,2},{3,3},{4,4},{5,5},{6,6},{7,7},{8,64},{9,65},{10,... | collective-permute-start | bytes 196616 | tf_op jit(solution)/shard_map/ppermute | solution.py:34
  141.0 39.6 %all-to-all-start.6 = ((bf16[16,4,64,128]{3,2,1,0:T(8,128)(2,1)}), bf16[16,4,64,128]{3,2,1,0:T(8,128)(2,1)S(1)}, u32[]{:S(2)}, u32[]{:S(2)}) async-start(bf16[16,4,64,128]{3,2,1,0:T(8,128)(2,1)} %broadcast_in_dim.35), calls=%async_computation.6 | async-start | bytes 2097152 | tf_op jit(solution)/shard_map/all_to_all | solution.py:16
Sparse Core Ops, SparseCore 0:
  89.7 64.3 all-gather.3

commit v2 on v1

v2 whole, which is shorter than its diff:
```python
import functools

import jax
import jax.numpy as jnp
from jax import lax
from jax.experimental import pallas as pl
from jax.experimental.pallas import tpu as pltpu
from jax.sharding import Mesh, PartitionSpec as P

SIZES = (4, 2, 4, 2, 2, 4)
AXES = ("zh", "co", "y", "xh", "xl", "zl")
DP = ("zh", "co")
STATE = ("y", "xh", "xl", "zl")
PLANE = ("y", "xh", "xl")
LINE = ("zh", "co", "zl")
GROUPS, SHARDS, PLANES, LINES = 8, 64, 16, 4
BF, F32 = jnp.bfloat16, jnp.float32


def exchange(blocks, axes):
    return lax.all_to_all(blocks, axes, 0, 0, tiled=True)


def spread(block, axes):
    return exchange(jnp.broadcast_to(block[None], (lax.axis_size(axes),) + block.shape), axes)


def swap_groups(block):
    pairs = []
    for source in range(512):
        zl, xl, xh = source % 4, source // 4 % 2, source // 8 % 2
        y, co, zh = source // 16 % 4, source // 64 % 2, source // 128
        pairs.append((source, ((((y * 2 + xh) * 4 + zh) * 2 + co) * 2 + xl) * 4 + zl))
    return lax.ppermute(block, AXES, pairs)


def call(body, outs, scratch=(), scalars=0, name=None, after=()):
    vmem, smem = pl.BlockSpec(memory_space=pltpu.VMEM), pl.BlockSpec(memory_space=pltpu.SMEM)

    def run(*args):
        def kernel(*refs):
            body(*refs[: len(args)], *refs[len(args) + len(after) :])

        return pl.pallas_call(
            kernel,
            out_shape=[jax.ShapeDtypeStruct(s, d) for s, d in outs],
            in_specs=[smem] * scalars + [vmem] * (len(args) - scalars)
            + [pl.BlockSpec(memory_space=pl.ANY)] * len(after),
            out_specs=[vmem] * len(outs),
            scratch_shapes=[pltpu.VMEM(s, d) for s, d in scratch],
            compiler_params=pltpu.CompilerParams(vmem_limit_bytes=24 << 20),
            name=name,
        )(*args, *after)

    return run


def put_split(ref, at, value):
    rows = value.shape[0]
    for part in range(3):
        piece = value.astype(BF)
        ref[at, part * rows + 64 : (part + 1) * rows + 64, :] = piece
        value = value - piece.astype(F32)


def to_rows(*columns):
    lane = lax.broadcasted_iota(jnp.int32, (64, 128), 1)
    table = jnp.zeros((64, 128), F32)
    for k, column in enumerate(columns):
        table = jnp.where(lane == k, column, table)
    rows = table.T[0:8, :]
    return jnp.concatenate([rows, jnp.zeros((8, 64), F32)], axis=1)


def to_columns(rows):
    return rows.T[0:64, :]


def start_body(emitted, backward, trans, out):
    weighted = (emitted[...] * backward[...]).astype(BF)
    for zl in range(LINES):
        out[zl, 0:64, :] = weighted
        sums = []
        for p in range(PLANES):
            s = p * LINES + zl
            block = trans[:, s * 128 : (s + 1) * 128].astype(F32)
            sums.append(jnp.sum(block, axis=0, keepdims=True))
        put_split(out, zl, jnp.concatenate(sums, axis=0))


def line_body(got, line, out):
    total = jnp.zeros((16, 128), F32)
    for zl in range(LINES):
        for part in range(3):
            total += got[zl, 64 + part * 16 : 80 + part * 16, :].astype(F32)
    pieces = []
    for part in range(3):
        piece = total.astype(BF)
        pieces.append(piece)
        total = total - piece.astype(F32)
    for zl in range(LINES):
        block = got[zl, 0:64, :]
        line[zl * 64 : (zl + 1) * 64, :] = block
        for p in range(PLANES):
            out[p, zl * 64 : (zl + 1) * 64, :] = block
    for p in range(PLANES):
        for part in range(3):
            out[p, 256 + part * 16 : 272 + part * 16, :] = pieces[part]


def propagate(got, trans, wide):
    for s in range(SHARDS):
        zl = s % LINES
        wide[:, s * 128 : (s + 1) * 128] = got[s // LINES, zl * 64 : (zl + 1) * 64, :]
    return lax.dot_general(
        wide[...], trans[...], (((1,), (1,)), ((), ())), preferred_element_type=F32
    )


def first_body(zl, got, trans, emitted, forward, out, post, wide):
    prop = propagate(got, trans, wide)
    sums = jnp.zeros((16, 128), F32)
    for p in range(PLANES):
        for part in range(3):
            sums += got[p, 256 + part * 16 : 272 + part * 16, :].astype(F32)
    scale = jnp.zeros((64, 128), F32)
    own = pl.multiple_of(zl[0] * 64, 64)
    for p in range(PLANES):
        scale += got[p, pl.ds(own, 64), :].astype(F32) * sums[p : p + 1, :]
    scale = jnp.sum(scale, axis=1, keepdims=True)
    peak = jnp.max(prop, axis=1, keepdims=True)
    out[0:64, :] = emitted[...] * (prop / peak)
    out[64:72, :] = to_rows(peak, scale)
    post[...] = jnp.broadcast_to(
        jnp.sum(forward[...] * prop, axis=1, keepdims=True), (64, 128)
    )


def round_body(width, got, line, out):
    infos = [to_columns(got[zl, 64:72, :]) for zl in range(LINES)]
    scale = (infos[0][:, 1:2] + infos[1][:, 1:2] + infos[2][:, 1:2] + infos[3][:, 1:2]) / width
    for zl in range(LINES):
        block = (got[zl, 0:64, :] * (infos[zl][:, 0:1] / scale)).astype(BF)
        line[zl * 64 : (zl + 1) * 64, :] = block
        for p in range(PLANES):
            out[p, zl * 64 : (zl + 1) * 64, :] = block


def second_body(got, trans, forward, post, far, prop_out, out, wide):
    prop = propagate(got, trans, wide)
    prop_out[...] = prop
    rows = to_rows(
        post[:, 0:1],
        jnp.sum(forward[...] * prop, axis=1, keepdims=True),
        jnp.sum(prop, axis=1, keepdims=True),
    )
    pieces = []
    for part in range(3):
        piece = rows.astype(BF)
        pieces.append(piece.astype(F32))
        rows = rows - pieces[-1]
    tail = jnp.concatenate(pieces + [jnp.zeros((8, 128), F32)], axis=0).astype(BF)
    for p in range(PLANES):
        out[p, 0:256, :] = far[...]
        out[p, 256:288, :] = tail


def sum_body(got, out):
    total = jnp.zeros((32, 128), F32)
    for p in range(PLANES):
        total += got[p, 256:288, :].astype(F32)
    total = total[0:8] + total[8:16] + total[16:24]
    for k in range(GROUPS * LINES):
        out[k] = total


def count_body(width, place, got, everyone, prop, late, early, backward, count, left, right):
    zh, co = place[0], place[1]
    own = zh * 2 + co
    mine = to_columns(jnp.sum(got[pl.ds(own * LINES, LINES)], axis=0) / width)
    backward[...] = prop[...] / mine[:, 2:3]
    for k in range(4):
        for c in range(2):
            g = lax.rem(zh + 4 - k, 4) * 2 + (co if c == 0 else 1 - co)
            sums = to_columns(jnp.sum(got[pl.ds(g * LINES, LINES)], axis=0) / width)
            for t, src in enumerate((late, early)):
                at = t * 512 + (k * 2 + c) * 64
                forward = everyone[g, 1 - t]
                left[at : at + 64, :] = (forward / sums[:, t : t + 1]).astype(BF)
                for p in range(2):
                    for zl in range(LINES):
                        shard = p * LINES + zl
                        right[at : at + 64, shard * 128 : (shard + 1) * 128] = src[
                            g * 2 + p, zl * 64 : (zl + 1) * 64, :
                        ]
    count[...] = jnp.dot(left[...].T, right[...], preferred_element_type=F32) * (1.0 / 1024)


def along(block, axis, step):
    size = lax.axis_size(axis)
    return lax.ppermute(block, axis, [(k, (k + step) % size) for k in range(size)])


def on_device(forward_probs, backward_last, emission, token_ids, transition):
    width = transition.shape[1]
    emitted = emission.at[token_ids.T.reshape(-1)].get(mode="promise_in_bounds")
    emitted = emitted.reshape(2, 64, 128)
    wide = [((64, 8192), BF)]

    (sent,) = call(start_body, [((4, 112, 128), BF)], name="start")(
        emitted[1], backward_last, transition
    )
    got = exchange(sent, "zl")
    line1, sent = call(line_body, [((256, 128), BF), ((16, 304, 128), BF)], name="line")(got)
    far1 = swap_groups(line1)
    forward_all = lax.all_gather(jnp.concatenate([forward_probs, forward_probs]), DP)
    got = exchange(sent, PLANE)
    zl = lax.axis_index("zl").reshape(1)
    sent, post1 = call(
        first_body,
        [((72, 128), F32), ((64, 128), F32)],
        wide,
        1,
        name="first",
        after=(far1,),
    )(zl, got, transition, emitted[0], forward_probs[1])
    late = lax.all_gather(far1, PLANE)
    got = spread(sent, "zl")
    line0, sent = call(
        functools.partial(round_body, width), [((256, 128), BF), ((16, 256, 128), BF)], name="round"
    )(got)
    far0 = swap_groups(line0)
    got = exchange(sent, PLANE)
    prop0, sent = call(
        second_body, [((64, 128), F32), ((16, 288, 128), BF)], wide, name="second"
    )(got, transition, forward_probs[0], post1, far0)
    early = exchange(sent, PLANE)
    (sent,) = call(sum_body, [((32, 8, 128), F32)], name="sums")(early)
    got = exchange(sent, LINE)
    place = jnp.stack([lax.axis_index("zh"), lax.axis_index("co")])
    return tuple(
        call(
            functools.partial(count_body, width),
            [((64, 128), F32), ((128, 1024), F32)],
            [((1024, 128), BF), ((1024, 1024), BF)],
            1,
            name="counts",
        )(place, got, forward_all, prop0, late, early)
    )


def solution(mesh):
    fine = Mesh(mesh.devices.reshape(SIZES), AXES)
    placed = (P(None, DP, STATE), P(DP, STATE), P(None, STATE), P(DP, None), P(STATE, None))
    return jax.shard_map(
        on_device,
        mesh=fine,
        in_specs=placed,
        out_specs=(P(DP, STATE), P(STATE, DP)),
        check_vma=False,
    )
```

time: 192 us -> 167 us (0.87)
  blocking collectives: 97.5 us -> 49.8 us
  waiting for transfers between devices: 16.8 us -> 39.8 us
  Pallas kernels: 0 us -> 8.59 us
  matrix products: 5.61 us -> 0 us
  other arithmetic: 4.72 us -> 0.74 us
    all_gather x1 -> x0, blocking collectives: 29.3 us -> none  [on_device(): forward_all = lax.all_gather(forward_probs, DP)]
    all_to_all x4 -> x3, blocking collectives: 68.1 us -> 49.8 us  [exchange(): return lax.all_to_all(blocks, axes, 0, 0, tiled=True)]
    ppermute x2, waiting for transfers between devices: 12.1 us -> 23.2 us  [swap_groups(): return lax.ppermute(block, AXES, pairs)]
    all_gather x1 -> x2, waiting for transfers between devices: 0.02 us -> 8.64 us  [the longest x1 8.64 us: on_device(): late = lax.all_gather(far1, PLANE)]
    pallas_call x0 -> x7, Pallas kernels: none -> 8.59 us  [run(): pl.pallas_call(kernel, out_shape=[jax.ShapeDtypeStruct(s, d) for s, d in...]
    dot_general x4 -> x0, matrix products: 5.61 us -> none  [the longest x2 3.05 us: on_device(): lax.dot_general(gathered, trans, (((0, 2), (1, 2)), ((), ())), preferred_...]
    unnamed x15 -> x20, local copies, waits for them, and re-layouts: 3.63 us -> 7.06 us
    broadcast_in_dim x7 -> x1, local copies, waits for them, and re-layouts: 3.04 us -> 0.01 us  [spread(): jnp.broadcast_to(block[None], (lax.axis_size(axes),) + block.shape)]
  transfers between devices with their start and end apart: 6 -> 7, of which waited for: 3 -> 4; matrix products, arithmetic and copies ran while one was open for 4% -> 0% of each run, Pallas kernels for 0% -> 3%
where the time goes in v2:
time: 167 us
  blocking collectives  49.8 us (30%)
  starting transfers between devices  44.9 us (27%)
  waiting for transfers between devices  39.8 us (24%)
  between operations  14.2 us (9%)
  Pallas kernels  8.59 us (5%)
  local copies, waits for them, and re-layouts  8.54 us (5%)
    all_to_all x3, blocking collectives, exchange(): return lax.all_to_all(blocks, axes, 0, 0, tiled=True)  49.8 us
    all_to_all x3, starting transfers between devices, exchange(): return lax.all_to_all(blocks, axes, 0, 0, tiled=True)  32.1 us
    ppermute x2, waiting for transfers between devices, swap_groups(): return lax.ppermute(block, AXES, pairs)  23.2 us
    ppermute x2, starting transfers between devices, swap_groups(): return lax.ppermute(block, AXES, pairs)  12.7 us
    all_gather x1, waiting for transfers between devices, on_device(): late = lax.all_gather(far1, PLANE)  8.64 us
    pallas_call x7, Pallas kernels, run(): pl.pallas_call(kernel, out_shape=[jax.ShapeDtypeStruct(s, d) for s, d in...  8.59 us
    all_to_all x3, waiting for transfers between devices, exchange(): return lax.all_to_all(blocks, axes, 0, 0, tiled=True)  7.3 us
    unnamed x20, local copies, waits for them, and re-layouts  7.06 us
  transfers between devices with their start and end apart: 7, of which 4 were waited for; matrix products, arithmetic and copies ran while one was open for 0% of the time, Pallas kernels for 3%

profile of v2, /device:TPU:1, one launch (start us, length us, event | category | flops | bytes accessed | tf_op | source)
XLA Modules:
  0.0 166.6 jit_solution(17192121196147518710)
XLA Ops:
  7.2 0.8 reshape.45
  8.0 0.2 copy-done
  8.2 0.6 gather_fusion
  8.9 1.6 copy-done.1
  10.5 0.8 copy-done.8
  11.2 0.3 start.1
  11.6 11.0 %all_to_all.30.refs_0_ = bf16[4,112,128]{2,1,0:T(8,128)(2,1)S(1)} all-to-all(bf16[4,112,128]{2,1,0:T(8,128)(2,1)S(1)} %start.1), channel_id=1, replica_groups=mesh['zh'=4,'co'=2,'y'=4,'xh'=2,'xl'=2,'zl'=4] {'zl'}, dimensions={0} | all-to-all | bytes 229376 | tf_op jit(solution)/shard_map/all_to_all | solution.py:21
  22.5 0.2 line.1
  22.7 1.0 copy-done.3
  23.8 7.0 %all-to-all-start.1 = ((bf16[16,304,128]{2,1,0:T(8,128)(2,1)}), bf16[16,304,128]{2,1,0:T(8,128)(2,1)}, u32[]{:S(2)}, u32[]{:S(2)}) async-start(bf16[16,304,128]{2,1,0:T(8,128)(2,1)} %copy-done.3), calls=%async_computation.1 | async-start | bytes 2490368 | tf_op jit(solution)/shard_map/all_to_all | solution.py:21
  30.8 0.6 pad_maximum_fusion
  31.5 7.3 %collective-permute-start = (bf16[256,128]{1,0:T(8,128)(2,1)S(1)}, bf16[256,128]{1,0:T(8,128)(2,1)S(1)}, u32[]{:S(2)}, u32[]{:S(2)}) collective-permute-start(bf16[256,128]{1,0:T(8,128)(2,1)S(1)} %get-tuple-element.11), channel_id=1, source_target_pairs={{0,0},{1,1},{2,2},{3,3},{4,4},{5,5},{6,6},{7,7},{8,64},{9,65},{10,... | collective-permute-start | bytes 196616 | tf_op jit(solution)/shard_map/ppermute | solution.py:34
  38.8 12.1 %collective-permute-done.refs_5_ = bf16[256,128]{1,0:T(8,128)(2,1)S(1)} collective-permute-done((bf16[256,128]{1,0:T(8,128)(2,1)S(1)}, bf16[256,128]{1,0:T(8,128)(2,1)S(1)}, u32[]{:S(2)}, u32[]{:S(2)}) %collective-permute-start) | collective-permute-done | bytes 65568 | tf_op jit(solution)/shard_map/ppermute | solution.py:34
  50.8 2.3 %first.1 = (f32[72,128]{1,0:T(8,128)S(1)}, f32[64,128]{1,0:T(8,128)S(1)}) custom-call(s32[1]{0:T(128)} %bitcast.2.refs_0_, bf16[16,304,128]{2,1,0:T(8,128)(2,1)} %all-to-all-done.1.refs_1_, bf16[128,8192]{1,0:T(8,128)(2,1)S(1)} %copy-done.2, f32[64,128]{1,0:T(8,128)S(1)} %get-tuple-element.20.refs_3_, f32[64,128]{1,0:T(8,128)S(1)} %get-tuple-element.19.refs_4_, ...), custom_call_target="tpu_custom_call" | custom-call | tf_op jit(solution)/shard_map/first/pallas_call | solution.py:44
  53.1 13.6 %all_to_all.31.refs_0_ = f32[4,72,128]{2,1,0:T(8,128)S(1)} all-to-all(f32[4,72,128]{2,1,0:T(8,128)S(1)} %broadcast_in_dim.2), channel_id=1, replica_groups=mesh['zh'=4,'co'=2,'y'=4,'xh'=2,'xl'=2,'zl'=4] {'zl'}, dimensions={0} | all-to-all | bytes 294912 | tf_op jit(solution)/shard_map/all_to_all | solution.py:21
  66.8 0.4 round.1
  67.1 1.0 copy-done.6
  68.1 8.6 %all-to-all-start.3 = ((bf16[16,256,128]{2,1,0:T(8,128)(2,1)}), bf16[16,256,128]{2,1,0:T(8,128)(2,1)}, u32[]{:S(2)}, u32[]{:S(2)}) async-start(bf16[16,256,128]{2,1,0:T(8,128)(2,1)} %copy-done.6), calls=%async_computation.3 | async-start | bytes 2097152 | tf_op jit(solution)/shard_map/all_to_all | solution.py:21
  76.8 0.0 all-gather.7.cloned.1.call-start
  76.8 0.7 all-gather.7.cloned.1.call-update
  77.5 5.4 %collective-permute-start.1 = (bf16[256,128]{1,0:T(8,128)(2,1)S(1)}, bf16[256,128]{1,0:T(8,128)(2,1)S(1)}, u32[]{:S(2)}, u32[]{:S(2)}) collective-permute-start(bf16[256,128]{1,0:T(8,128)(2,1)S(1)} %get-tuple-element.15), channel_id=1, source_target_pairs={{0,0},{1,1},{2,2},{3,3},{4,4},{5,5},{6,6},{7,7},{8,64},{9,65},{10,... | collective-permute-start | bytes 196616 | tf_op jit(solution)/shard_map/ppermute | solution.py:34
  83.0 11.1 %collective-permute-done.1.refs_4_ = bf16[256,128]{1,0:T(8,128)(2,1)S(1)} collective-permute-done((bf16[256,128]{1,0:T(8,128)(2,1)S(1)}, bf16[256,128]{1,0:T(8,128)(2,1)S(1)}, u32[]{:S(2)}, u32[]{:S(2)}) %collective-permute-start.1) | collective-permute-done | bytes 65568 | tf_op jit(solution)/shard_map/ppermute | solution.py:34
  94.1 2.3 %second.1 = (f32[64,128]{1,0:T(8,128)S(1)}, bf16[16,288,128]{2,1,0:T(8,128)(2,1)S(1)}) custom-call(bf16[16,256,128]{2,1,0:T(8,128)(2,1)} %all-to-all-done.3.refs_0_, bf16[128,8192]{1,0:T(8,128)(2,1)S(1)} %copy-done.2, f32[64,128]{1,0:T(8,128)S(1)} %get-tuple-element.18.refs_2_, f32[64,128]{1,0:T(8,128)S(1)} %get-tuple-element.14.refs_3_, ...), custom_call_target="tpu_custom_call" | custom-call | tf_op jit(solution)/shard_map/second/pallas_call | solution.py:44
  96.4 25.2 %all_to_all.32.refs_0_.refs_5_ = bf16[16,288,128]{2,1,0:T(8,128)(2,1)S(1)} all-to-all(bf16[16,288,128]{2,1,0:T(8,128)(2,1)S(1)} %get-tuple-element.16), channel_id=1, replica_groups=mesh['zh'=4,'co'=2,'y'=4,'xh'=2,'xl'=2,'zl'=4] {'y','xh','xl'}, dimensions={0} | all-to-all | bytes 2359296 | tf_op jit(solution)/shard_map/all_to_all | solution.py:21
  121.6 0.7 sums.1
  122.3 16.5 %all-to-all-start.5 = ((f32[32,8,128]{2,1,0:T(8,128)}), f32[32,8,128]{2,1,0:T(8,128)S(1)}, u32[]{:S(2)}, u32[]{:S(2)}) async-start(f32[32,8,128]{2,1,0:T(8,128)} %sums.1), calls=%async_computation.5 | async-start | bytes 262144 | tf_op jit(solution)/shard_map/all_to_all | solution.py:21
  138.9 0.1 pad_add_fusion.refs_0_
  138.9 8.6 %all-gather.7.cloned.1.call-done = bf16[4096,128]{1,0:T(8,128)(2,1)} async-done(((bf16[256,128]{1,0:T(8,128)(2,1)}), bf16[4096,128]{1,0:T(8,128)(2,1)}) %all-gather.7.cloned.1.call-update) | async-done | bytes 1048592 | tf_op jit(solution)/shard_map/all_gather | solution.py:227
  147.6 7.3 %all-to-all-done.5.refs_1_ = f32[32,8,128]{2,1,0:T(8,128)S(1)} async-done(((f32[32,8,128]{2,1,0:T(8,128)}), f32[32,8,128]{2,1,0:T(8,128)S(1)}, u32[]{:S(2)}, u32[]{:S(2)}) %all-to-all-start.5) | async-done | bytes 131104 | tf_op jit(solution)/shard_map/all_to_all | solution.py:21
  154.9 1.2 copy-done.4
  156.1 1.2 copy-done.5
  157.3 2.4 %counts.1 = (f32[64,128]{1,0:T(8,128)}, f32[128,1024]{1,0:T(8,128)}) custom-call(s32[2]{0:T(128)S(1)} %pad_add_fusion.refs_0_, f32[32,8,128]{2,1,0:T(8,128)S(1)} %all-to-all-done.5.refs_1_, f32[8,4,64,128]{3,2,1,0:T(8,128)S(1)} %bitcast.12, f32[64,128]{1,0:T(8,128)S(1)} %get-tuple-element.17.refs_3_, bf16[16,256,128]{2,1,0:T(8,128)(2,1)S(1)} %bitcast.13, ...), custom_call_target="tpu_custom_call" | custom-call | tf_op jit(solution)/shard_map/counts/pallas_call | solution.py:44
  (23 shorter events, 0.1 us)
Async XLA Ops:
  7.2 1.1 copy-start
  8.9 1.6 copy-start.1
  10.5 0.8 copy-start.8
  22.7 1.0 copy-start.3
  23.7 7.0 %copy-start.9 = (f32[2,64,128]{2,1,0:T(8,128)S(1)}, f32[2,64,128]{2,1,0:T(8,128)}, u32[]{:S(2)}) copy-start(f32[2,64,128]{2,1,0:T(8,128)} %param.5) | copy-start | bytes 196612
  23.8 27.1 %copy-start.2 = (bf16[128,8192]{1,0:T(8,128)(2,1)S(1)}, bf16[128,8192]{1,0:T(8,128)(2,1)}, u32[]{:S(2)}) copy-start(bf16[128,8192]{1,0:T(8,128)(2,1)} %refs_1_.3) | copy-start | bytes 6291460
  23.8 27.1 %all-to-all-start.1 = ((bf16[16,304,128]{2,1,0:T(8,128)(2,1)}), bf16[16,304,128]{2,1,0:T(8,128)(2,1)}, u32[]{:S(2)}, u32[]{:S(2)}) async-start(bf16[16,304,128]{2,1,0:T(8,128)(2,1)} %copy-done.3), calls=%async_computation.1 | async-start | bytes 2490368 | tf_op jit(solution)/shard_map/all_to_all | solution.py:21
  30.7 108.2 %all-gather.5.cloned.1.call-start = ((), (), s32[]{:S(2)}) async-start(), calls=%async_computation.6 | async-start | bytes 1179648 | tf_op jit(solution)/shard_map/all_gather | solution.py:216
  31.5 19.4 %collective-permute-start = (bf16[256,128]{1,0:T(8,128)(2,1)S(1)}, bf16[256,128]{1,0:T(8,128)(2,1)S(1)}, u32[]{:S(2)}, u32[]{:S(2)}) collective-permute-start(bf16[256,128]{1,0:T(8,128)(2,1)S(1)} %get-tuple-element.11), channel_id=1, source_target_pairs={{0,0},{1,1},{2,2},{3,3},{4,4},{5,5},{6,6},{7,7},{8,64},{9,65},{10,... | collective-permute-start | bytes 196616 | tf_op jit(solution)/shard_map/ppermute | solution.py:34
  50.8 2.3 %copy-start.7 = (bf16[256,128]{1,0:T(8,128)(2,1)}, bf16[256,128]{1,0:T(8,128)(2,1)S(1)}, u32[]{:S(2)}) copy-start(bf16[256,128]{1,0:T(8,128)(2,1)S(1)} %collective-permute-done.refs_5_) | copy-start | bytes 196612
  67.1 1.0 copy-start.6
  68.1 25.9 %all-to-all-start.3 = ((bf16[16,256,128]{2,1,0:T(8,128)(2,1)}), bf16[16,256,128]{2,1,0:T(8,128)(2,1)}, u32[]{:S(2)}, u32[]{:S(2)}) async-start(bf16[16,256,128]{2,1,0:T(8,128)(2,1)} %copy-done.6), calls=%async_computation.3 | async-start | bytes 2097152 | tf_op jit(solution)/shard_map/all_to_all | solution.py:21
  76.8 70.8 %all-gather.7.cloned.1.call-start = ((), (), s32[]{:S(2)}) async-start(), calls=%async_computation.7 | async-start | bytes 1114112 | tf_op jit(solution)/shard_map/all_gather | solution.py:227
  77.5 16.6 %collective-permute-start.1 = (bf16[256,128]{1,0:T(8,128)(2,1)S(1)}, bf16[256,128]{1,0:T(8,128)(2,1)S(1)}, u32[]{:S(2)}, u32[]{:S(2)}) collective-permute-start(bf16[256,128]{1,0:T(8,128)(2,1)S(1)} %get-tuple-element.15), channel_id=1, source_target_pairs={{0,0},{1,1},{2,2},{3,3},{4,4},{5,5},{6,6},{7,7},{8,64},{9,65},{10,... | collective-permute-start | bytes 196616 | tf_op jit(solution)/shard_map/ppermute | solution.py:34
  122.3 32.6 %all-to-all-start.5 = ((f32[32,8,128]{2,1,0:T(8,128)}), f32[32,8,128]{2,1,0:T(8,128)S(1)}, u32[]{:S(2)}, u32[]{:S(2)}) async-start(f32[32,8,128]{2,1,0:T(8,128)} %sums.1), calls=%async_computation.5 | async-start | bytes 262144 | tf_op jit(solution)/shard_map/all_to_all | solution.py:21
  154.9 1.2 copy-start.4
  156.1 1.2 copy-start.5
Sparse Core Ops, SparseCore 0:
  33.7 52.2 all-gather.4
  89.0 58.4 all-gather.6

commit v3 on v2

v3 whole, which is shorter than its diff:
```python
import functools

import jax
import jax.numpy as jnp
from jax import lax
from jax.experimental import pallas as pl
from jax.experimental.pallas import tpu as pltpu
from jax.sharding import Mesh, PartitionSpec as P

SIZES = (4, 2, 4, 2, 2, 4)
AXES = ("zh", "co", "y", "xh", "xl", "zl")
DP = ("zh", "co")
STATE = ("y", "xh", "xl", "zl")
PLANE = ("y", "xh", "xl")
LINE = ("zh", "co", "zl")
GROUPS, SHARDS, PLANES, LINES = 8, 64, 16, 4
BF, F32 = jnp.bfloat16, jnp.float32


def exchange(blocks, axes):
    return lax.all_to_all(blocks, axes, 0, 0, tiled=True)


def spread(block, axes):
    return exchange(jnp.broadcast_to(block[None], (lax.axis_size(axes),) + block.shape), axes)


def swap_groups(block):
    pairs = []
    for source in range(512):
        zl, xl, xh = source % 4, source // 4 % 2, source // 8 % 2
        y, co, zh = source // 16 % 4, source // 64 % 2, source // 128
        pairs.append((source, ((((y * 2 + xh) * 4 + zh) * 2 + co) * 2 + xl) * 4 + zl))
    return lax.ppermute(block, AXES, pairs)


PLACES = {
    "vmem": pl.BlockSpec(memory_space=pltpu.VMEM),
    "smem": pl.BlockSpec(memory_space=pltpu.SMEM),
    "any": pl.BlockSpec(memory_space=pl.ANY),
    "hbm": pl.BlockSpec(memory_space=pltpu.HBM),
}


def call(name, body, args, outs, scratch=(), after=(), limit=24):
    def kernel(*refs):
        body(*refs[: len(args)], *refs[len(args) + len(after) :])

    return pl.pallas_call(
        kernel,
        out_shape=[jax.ShapeDtypeStruct(s, d) for s, d, _ in outs],
        in_specs=[PLACES[place] for place, _ in args] + [PLACES["any"]] * len(after),
        out_specs=[PLACES[place] for _, _, place in outs],
        scratch_shapes=list(scratch),
        compiler_params=pltpu.CompilerParams(vmem_limit_bytes=limit << 20),
        name=name,
    )(*[array for _, array in args], *after)


def split3(value):
    pieces = []
    for _ in range(3):
        pieces.append(value.astype(BF))
        value = value - pieces[-1].astype(F32)
    return pieces


def to_rows(*columns):
    lane = lax.broadcasted_iota(jnp.int32, (64, 128), 1)
    table = jnp.zeros((64, 128), F32)
    for k, column in enumerate(columns):
        table = jnp.where(lane == k, column, table)
    rows = table.T[0:8, :]
    return jnp.concatenate([rows, jnp.zeros((8, 64), F32)], axis=1)


def to_columns(rows):
    return rows.T[0:64, :]


def start_body(tokens, emission, backward, trans, out, emitted, rows, now, held, sems):
    width = trans.shape[1] // LINES
    copies = [
        pltpu.make_async_copy(emission, rows, sems.at[LINES]),
        pltpu.make_async_copy(backward, now, sems.at[LINES + 1]),
    ]
    for k in range(LINES):
        part = pl.ds(k * width, width)
        copies.append(pltpu.make_async_copy(trans.at[:, part], held.at[:, part], sems.at[k]))
    for copy in copies:
        copy.start()
    copies[0].wait()
    for b in range(64):
        emitted[b : b + 1, :] = rows[pl.ds(tokens[1, b], 1), :]
    copies[1].wait()
    weighted = (emitted[...] * now[...]).astype(BF)
    for b in range(64):
        emitted[b : b + 1, :] = rows[pl.ds(tokens[0, b], 1), :]
    sums = [[] for _ in range(LINES)]
    for k in range(LINES):
        copies[2 + k].wait()
        for s in range(k * 16, k * 16 + 16):
            block = held[:, s * 128 : (s + 1) * 128].astype(F32)
            sums[s % LINES].append(jnp.sum(block, axis=0, keepdims=True))
    for zl in range(LINES):
        out[zl, 0:64, :] = weighted
        for part, piece in enumerate(split3(jnp.concatenate(sums[zl], axis=0))):
            out[zl, 64 + part * 16 : 80 + part * 16, :] = piece


def line_body(got, line, out):
    total = jnp.zeros((16, 128), F32)
    for zl in range(LINES):
        for part in range(3):
            total += got[zl, 64 + part * 16 : 80 + part * 16, :].astype(F32)
    pieces = split3(total)
    for zl in range(LINES):
        block = got[zl, 0:64, :]
        line[zl * 64 : (zl + 1) * 64, :] = block
        for p in range(PLANES):
            out[p, zl * 64 : (zl + 1) * 64, :] = block
    for p in range(PLANES):
        for part in range(3):
            out[p, 256 + part * 16 : 272 + part * 16, :] = pieces[part]


def propagate(got, trans, wide):
    for s in range(SHARDS):
        zl = s % LINES
        wide[:, s * 128 : (s + 1) * 128] = got[s // LINES, zl * 64 : (zl + 1) * 64, :]
    return lax.dot_general(
        wide[...], trans[...], (((1,), (1,)), ((), ())), preferred_element_type=F32
    )


def first_body(zl, got, trans, emitted, forward, out, post, wide):
    prop = propagate(got, trans, wide)
    sums = jnp.zeros((16, 128), F32)
    for p in range(PLANES):
        for part in range(3):
            sums += got[p, 256 + part * 16 : 272 + part * 16, :].astype(F32)
    scale = jnp.zeros((64, 128), F32)
    own = pl.multiple_of(zl[0] * 64, 64)
    for p in range(PLANES):
        scale += got[p, pl.ds(own, 64), :].astype(F32) * sums[p : p + 1, :]
    scale = jnp.sum(scale, axis=1, keepdims=True)
    peak = jnp.max(prop, axis=1, keepdims=True)
    value, info = emitted[...] * (prop / peak), to_rows(peak, scale)
    for k in range(LINES):
        out[k, 0:64, :] = value
        out[k, 64:72, :] = info
    post[...] = jnp.broadcast_to(
        jnp.sum(forward[...] * prop, axis=1, keepdims=True), (64, 128)
    )


def round_body(width, got, far, line, out):
    infos = [to_columns(got[zl, 64:72, :]) for zl in range(LINES)]
    scale = (infos[0][:, 1:2] + infos[1][:, 1:2] + infos[2][:, 1:2] + infos[3][:, 1:2]) / width
    for zl in range(LINES):
        block = (got[zl, 0:64, :] * (infos[zl][:, 0:1] / scale)).astype(BF)
        line[zl * 64 : (zl + 1) * 64, :] = block
        for p in range(PLANES):
            out[p, zl * 64 : (zl + 1) * 64, :] = block
    for p in range(PLANES):
        out[p, 256:512, :] = far[...]


def second_body(got, trans, forward, post, far, prop_out, out, wide):
    prop = propagate(got, trans, wide)
    prop_out[...] = prop
    rows = to_rows(
        post[:, 0:1],
        jnp.sum(forward[...] * prop, axis=1, keepdims=True),
        jnp.sum(prop, axis=1, keepdims=True),
    )
    pieces = [piece.astype(F32) for piece in split3(rows)]
    tail = jnp.concatenate(pieces + [jnp.zeros((8, 128), F32)], axis=0).astype(BF)
    for p in range(PLANES):
        out[p, 0:256, :] = far[...]
        out[p, 256:288, :] = tail


def sum_body(got, out):
    total = jnp.zeros((32, 128), F32)
    for p in range(PLANES):
        total += got[p, 256:288, :].astype(F32)
    total = total[0:8] + total[8:16] + total[16:24]
    both = total[0:1] + pltpu.roll(total[1:2], 64, axis=1)
    pair = jnp.concatenate([both, total[2:3]], axis=0)
    for k in range(GROUPS * LINES):
        out[k] = pair


def prepare_body(late, early, forward, right, held, sems):
    copies = []
    for g in range(GROUPS):
        copies.append(pltpu.make_async_copy(forward.at[g, pl.ds(0, 2)], held.at[g], sems.at[g]))
        copies[-1].start()
    for t, (src, first) in enumerate(((late, 256), (early, 0))):
        for g in range(GROUPS):
            at = t * 512 + g * 64
            for c in range(GROUPS):
                rows = first + c % LINES * 64
                right[at : at + 64, c * 128 : (c + 1) * 128] = src[
                    g * 2 + c // LINES, rows : rows + 64, :
                ]
    for copy in copies:
        copy.wait()


def count_body(width, group, got, forward, prop, right, backward, count, left):
    def columns(first):
        pair = jnp.sum(got[pl.ds(first, LINES)], axis=0) / width
        table = jnp.concatenate([pair, jnp.zeros((6, 128), F32)], axis=0).T
        return table[0:64, 0:1], table[64:128, 0:1], table[0:64, 1:2]

    backward[...] = prop[...] / columns(group[0] * LINES)[2]
    for g in range(GROUPS):
        post = columns(g * LINES)
        for t in range(2):
            at = t * 512 + g * 64
            left[at : at + 64, :] = (forward[g, 1 - t] / post[t]).astype(BF)
    count[...] = jnp.dot(left[...].T, right[...], preferred_element_type=F32) * (1.0 / 1024)


def on_device(forward_probs, backward_last, emission, token_ids, transition):
    width = transition.shape[1]
    wide = pltpu.VMEM((64, 8192), BF)

    forward_all = lax.all_gather(jnp.concatenate([forward_probs, forward_probs]), DP)
    sent, emitted = call(
        "start",
        start_body,
        [("smem", token_ids.T), ("hbm", emission), ("hbm", backward_last), ("hbm", transition)],
        [((4, 112, 128), BF, "vmem"), ((64, 128), F32, "vmem")],
        [
            pltpu.VMEM(emission.shape, F32),
            pltpu.VMEM((64, 128), F32),
            pltpu.VMEM((128, 8192), BF),
            pltpu.SemaphoreType.DMA((LINES + 2,)),
        ],
        limit=60,
    )
    got = exchange(sent, "zl")
    line1, sent = call(
        "line",
        line_body,
        [("vmem", got)],
        [((256, 128), BF, "vmem"), ((16, 304, 128), BF, "vmem")],
    )
    far1 = swap_groups(line1)
    got = exchange(sent, PLANE)
    sent, post1 = call(
        "first",
        first_body,
        [
            ("smem", lax.axis_index("zl").reshape(1)),
            ("vmem", got),
            ("vmem", transition),
            ("vmem", emitted),
            ("vmem", forward_probs[1]),
        ],
        [((4, 72, 128), F32, "vmem"), ((64, 128), F32, "vmem")],
        [wide],
        (far1,),
    )
    got = exchange(sent, "zl")
    line0, sent = call(
        "round",
        functools.partial(round_body, width),
        [("vmem", got), ("vmem", far1)],
        [((256, 128), BF, "vmem"), ((16, 512, 128), BF, "vmem")],
    )
    far0 = swap_groups(line0)
    got = exchange(sent, PLANE)
    prop0, sent = call(
        "second",
        second_body,
        [("vmem", got), ("vmem", transition), ("vmem", forward_probs[0]), ("vmem", post1)]
        + [("vmem", far0)],
        [((64, 128), F32, "vmem"), ((16, 288, 128), BF, "vmem")],
        [wide],
    )
    early = exchange(sent, PLANE)
    (sent,) = call("sums", sum_body, [("vmem", early)], [((32, 2, 128), F32, "vmem")])
    right, forward = call(
        "prepare",
        prepare_body,
        [("vmem", got), ("vmem", early), ("any", forward_all)],
        [((1024, 1024), BF, "vmem"), ((8, 2, 64, 128), F32, "vmem")],
        [pltpu.SemaphoreType.DMA((GROUPS,))],
    )
    got = exchange(sent, LINE)
    group = lax.axis_index(DP).reshape(1)
    return tuple(
        call(
            "counts",
            functools.partial(count_body, width),
            [("smem", group), ("vmem", got), ("vmem", forward), ("vmem", prop0), ("vmem", right)],
            [((64, 128), F32, "vmem"), ((128, 1024), F32, "vmem")],
            [pltpu.VMEM((1024, 128), BF)],
        )
    )


def solution(mesh):
    fine = Mesh(mesh.devices.reshape(SIZES), AXES)
    placed = (P(None, DP, STATE), P(DP, STATE), P(None, STATE), P(DP, None), P(STATE, None))
    return jax.shard_map(
        on_device,
        mesh=fine,
        in_specs=placed,
        out_specs=(P(DP, STATE), P(STATE, DP)),
        check_vma=False,
    )
```

time: 167 us -> 160 us (0.958)
  blocking collectives: 49.8 us -> 39.4 us
  Pallas kernels: 8.59 us -> 13.3 us
    all_to_all x3, blocking collectives: 49.8 us -> 39.4 us  [exchange(): return lax.all_to_all(blocks, axes, 0, 0, tiled=True)]
    ppermute x2, waiting for transfers between devices: 23.2 us -> 32.7 us  [swap_groups(): return lax.ppermute(block, AXES, pairs)]
    all_gather x1 -> x0, waiting for transfers between devices: 8.64 us -> none  [on_device(): late = lax.all_gather(far1, PLANE)]
    pallas_call x7 -> x8, Pallas kernels: 8.59 us -> 13.3 us  [call(): pl.pallas_call(kernel, out_shape=[jax.ShapeDtypeStruct(s, d) for s, d, _...]
    ppermute x2, starting transfers between devices: 12.7 us -> 16.5 us  [swap_groups(): return lax.ppermute(block, AXES, pairs)]
    all_to_all x3, starting transfers between devices: 32.1 us -> 28.7 us  [exchange(): return lax.all_to_all(blocks, axes, 0, 0, tiled=True)]
    unnamed x20 -> x16, local copies, waits for them, and re-layouts: 7.06 us -> 6.51 us
  transfers between devices with their start and end apart: 7 -> 6, of which waited for: 4 -> 3; matrix products, arithmetic and copies ran while one was open for 0% -> 1% of each run, Pallas kernels for 3% -> 4%
where the time goes in v3:
time: 160 us
  starting transfers between devices  45.2 us (28%)
  waiting for transfers between devices  39.6 us (25%)
  blocking collectives  39.4 us (25%)
  between operations  14.2 us (9%)
  Pallas kernels  13.3 us (8%)
  local copies, waits for them, and re-layouts  7.29 us (5%)
    all_to_all x3, blocking collectives, exchange(): return lax.all_to_all(blocks, axes, 0, 0, tiled=True)  39.4 us
    ppermute x2, waiting for transfers between devices, swap_groups(): return lax.ppermute(block, AXES, pairs)  32.7 us
    all_to_all x3, starting transfers between devices, exchange(): return lax.all_to_all(blocks, axes, 0, 0, tiled=True)  28.7 us
    ppermute x2, starting transfers between devices, swap_groups(): return lax.ppermute(block, AXES, pairs)  16.5 us
    pallas_call x8, Pallas kernels, call(): pl.pallas_call(kernel, out_shape=[jax.ShapeDtypeStruct(s, d) for s, d, _...  13.3 us
    all_to_all x3, waiting for transfers between devices, exchange(): return lax.all_to_all(blocks, axes, 0, 0, tiled=True)  6.82 us
    unnamed x16, local copies, waits for them, and re-layouts  6.51 us
  transfers between devices with their start and end apart: 6, of which 3 were waited for; matrix products, arithmetic and copies ran while one was open for 1% of the time, Pallas kernels for 4%

profile of v3, /device:TPU:1, one launch (start us, length us, event | category | flops | bytes accessed | tf_op | source)
XLA Modules:
  0.0 159.7 jit_solution(8551678751337499339)
XLA Ops:
  7.2 3.2 %start.1 = (bf16[4,112,128]{2,1,0:T(8,128)(2,1)}, f32[64,128]{1,0:T(8,128)}) custom-call(s32[2,64]{1,0:T(2,128)} %bitcast.9, f32[1024,128]{1,0:T(8,128)} %refs_1_.2, f32[64,128]{1,0:T(8,128)} %refs_2_.2, bf16[128,8192]{1,0:T(8,128)(2,1)} %refs_1_.3), custom_call_target="tpu_custom_call" | custom-call | tf_op jit(solution)/shard_map/start/pallas_call | solution.py:49
  10.4 0.0 copy-start
  10.4 0.0 copy-start.6
  10.4 11.3 %all_to_all.30.refs_0_ = bf16[4,112,128]{2,1,0:T(8,128)(2,1)S(1)} all-to-all(bf16[4,112,128]{2,1,0:T(8,128)(2,1)} %get-tuple-element.14), channel_id=1, replica_groups=mesh['zh'=4,'co'=2,'y'=4,'xh'=2,'xl'=2,'zl'=4] {'zl'}, dimensions={0} | all-to-all | bytes 229376 | tf_op jit(solution)/shard_map/all_to_all | solution.py:21
  21.7 0.8 line.1
  22.5 1.1 copy-done.4
  23.5 6.8 %all-to-all-start.1 = ((bf16[16,304,128]{2,1,0:T(8,128)(2,1)}), bf16[16,304,128]{2,1,0:T(8,128)(2,1)S(1)}, u32[]{:S(2)}, u32[]{:S(2)}) async-start(bf16[16,304,128]{2,1,0:T(8,128)(2,1)} %copy-done.4), calls=%async_computation.1 | async-start | bytes 2490368 | tf_op jit(solution)/shard_map/all_to_all | solution.py:21
  30.3 7.3 %collective-permute-start = (bf16[256,128]{1,0:T(8,128)(2,1)}, bf16[256,128]{1,0:T(8,128)(2,1)S(1)}, u32[]{:S(2)}, u32[]{:S(2)}) collective-permute-start(bf16[256,128]{1,0:T(8,128)(2,1)} %get-tuple-element.17), channel_id=1, source_target_pairs={{0,0},{1,1},{2,2},{3,3},{4,4},{5,5},{6,6},{7,7},{8,64},{9,65},{10,... | collective-permute-start | bytes 196616 | tf_op jit(solution)/shard_map/ppermute | solution.py:34
  37.6 0.8 slice_bitcast_fusion
  38.4 12.2 %collective-permute-done.refs_5_.refs_1_ = bf16[256,128]{1,0:T(8,128)(2,1)S(1)} collective-permute-done((bf16[256,128]{1,0:T(8,128)(2,1)}, bf16[256,128]{1,0:T(8,128)(2,1)S(1)}, u32[]{:S(2)}, u32[]{:S(2)}) %collective-permute-start) | collective-permute-done | bytes 65568 | tf_op jit(solution)/shard_map/ppermute | solution.py:34
  50.7 0.0 all-to-all-done.1.refs_1_
  50.7 1.0 first.1
  51.7 8.2 %all_to_all.31.refs_0_ = f32[4,72,128]{2,1,0:T(8,128)S(1)} all-to-all(f32[4,72,128]{2,1,0:T(8,128)S(1)} %get-tuple-element.18), channel_id=1, replica_groups=mesh['zh'=4,'co'=2,'y'=4,'xh'=2,'xl'=2,'zl'=4] {'zl'}, dimensions={0} | all-to-all | bytes 294912 | tf_op jit(solution)/shard_map/all_to_all | solution.py:21
  59.8 0.4 round.1
  60.3 1.3 copy-done.1
  61.6 6.8 %all-to-all-start.3 = ((bf16[16,512,128]{2,1,0:T(8,128)(2,1)}), bf16[16,512,128]{2,1,0:T(8,128)(2,1)}, u32[]{:S(2)}, u32[]{:S(2)}) async-start(bf16[16,512,128]{2,1,0:T(8,128)(2,1)} %copy-done.1), calls=%async_computation.3 | async-start | bytes 4194304 | tf_op jit(solution)/shard_map/all_to_all | solution.py:21
  68.4 0.0 all-gather.3.cloned.1.call-start
  68.5 0.7 pad_maximum_fusion
  69.1 0.0 all-gather.3.cloned.1.call-update
  69.1 9.2 %collective-permute-start.1 = (bf16[256,128]{1,0:T(8,128)(2,1)S(1)}, bf16[256,128]{1,0:T(8,128)(2,1)S(1)}, u32[]{:S(2)}, u32[]{:S(2)}) collective-permute-start(bf16[256,128]{1,0:T(8,128)(2,1)S(1)} %get-tuple-element.21), channel_id=1, source_target_pairs={{0,0},{1,1},{2,2},{3,3},{4,4},{5,5},{6,6},{7,7},{8,64},{9,65},{10,... | collective-permute-start | bytes 196616 | tf_op jit(solution)/shard_map/ppermute | solution.py:34
  78.3 20.5 %collective-permute-done.1.refs_4_ = bf16[256,128]{1,0:T(8,128)(2,1)S(1)} collective-permute-done((bf16[256,128]{1,0:T(8,128)(2,1)S(1)}, bf16[256,128]{1,0:T(8,128)(2,1)S(1)}, u32[]{:S(2)}, u32[]{:S(2)}) %collective-permute-start.1) | collective-permute-done | bytes 65568 | tf_op jit(solution)/shard_map/ppermute | solution.py:34
  98.8 2.7 %second.1 = (f32[64,128]{1,0:T(8,128)S(1)}, bf16[16,288,128]{2,1,0:T(8,128)(2,1)S(1)}) custom-call(bf16[16,512,128]{2,1,0:T(8,128)(2,1)} %all-to-all-done.3.refs_0_, bf16[128,8192]{1,0:T(8,128)(2,1)S(1)} %copy-done, f32[64,128]{1,0:T(8,128)S(1)} %get-tuple-element.26.refs_2_, f32[64,128]{1,0:T(8,128)S(1)} %get-tuple-element.20.refs_3_, ...), custom_call_target="tpu_custom_call" | custom-call | tf_op jit(solution)/shard_map/second/pallas_call | solution.py:49
  101.5 19.9 %all_to_all.32.refs_0_.refs_1_ = bf16[16,288,128]{2,1,0:T(8,128)(2,1)S(1)} all-to-all(bf16[16,288,128]{2,1,0:T(8,128)(2,1)S(1)} %get-tuple-element.22), channel_id=1, replica_groups=mesh['zh'=4,'co'=2,'y'=4,'xh'=2,'xl'=2,'zl'=4] {'y','xh','xl'}, dimensions={0} | all-to-all | bytes 2359296 | tf_op jit(solution)/shard_map/all_to_all | solution.py:21
  121.5 0.7 sums.1
  122.2 15.1 %all-to-all-start.5 = ((f32[32,2,128]{2,1,0:T(2,128)}), f32[32,2,128]{2,1,0:T(2,128)S(1)}, u32[]{:S(2)}, u32[]{:S(2)}) async-start(f32[32,2,128]{2,1,0:T(2,128)} %sums.1), calls=%async_computation.5 | async-start | bytes 65536 | tf_op jit(solution)/shard_map/all_to_all | solution.py:21
  137.3 0.0 all-gather.3.cloned.1.call-done
  137.3 1.2 copy-done.5
  138.5 2.7 %prepare.1 = (bf16[1024,1024]{1,0:T(8,128)(2,1)S(1)}, f32[8,2,64,128]{3,2,1,0:T(8,128)S(1)}) custom-call(bf16[16,512,128]{2,1,0:T(8,128)(2,1)} %all-to-all-done.3.refs_0_, bf16[16,288,128]{2,1,0:T(8,128)(2,1)S(1)} %all_to_all.32.refs_0_.refs_1_, f32[8,4,64,128]{3,2,1,0:T(8,128)S(1)} %bitcast.8), custom_call_target="tpu_custom_call" | custom-call | tf_op jit(solution)/shard_map/prepare/pallas_call | solution.py:49
  141.3 1.3 copy-done.2
  142.6 6.8 %all-to-all-done.5.refs_1_ = f32[32,2,128]{2,1,0:T(2,128)S(1)} async-done(((f32[32,2,128]{2,1,0:T(2,128)}), f32[32,2,128]{2,1,0:T(2,128)S(1)}, u32[]{:S(2)}, u32[]{:S(2)}) %all-to-all-start.5) | async-done | bytes 32800 | tf_op jit(solution)/shard_map/all_to_all | solution.py:21
  149.4 1.6 copy-done.3
  151.0 1.8 %counts.1 = (f32[64,128]{1,0:T(8,128)}, f32[128,1024]{1,0:T(8,128)}) custom-call(s32[1]{0:T(128)} %bitcast.refs_0_, f32[32,2,128]{2,1,0:T(2,128)S(1)} %all-to-all-done.5.refs_1_, f32[8,2,64,128]{3,2,1,0:T(8,128)S(1)} %get-tuple-element.23.refs_2_, f32[64,128]{1,0:T(8,128)S(1)} %get-tuple-element.24.refs_3_, bf16[1024,1024]{1,0:T(8,128)(2,1)S(1)} %copy-done.3), custom_call_target="tpu_custom_call" | custom-call | tf_op jit(solution)/shard_map/counts/pallas_call | solution.py:49
  (10 shorter events, 0.0 us)
Async XLA Ops:
  10.4 40.3 %copy-start = (bf16[128,8192]{1,0:T(8,128)(2,1)S(1)}, bf16[128,8192]{1,0:T(8,128)(2,1)}, u32[]{:S(2)}) copy-start(bf16[128,8192]{1,0:T(8,128)(2,1)} %refs_1_.3) | copy-start | bytes 6291460
  10.4 40.3 %copy-start.6 = (f32[64,128]{1,0:T(8,128)S(1)}, f32[64,128]{1,0:T(8,128)}, u32[]{:S(2)}) copy-start(f32[64,128]{1,0:T(8,128)} %get-tuple-element.16.refs_3_) | copy-start | bytes 98308
  22.5 1.1 copy-start.4
  23.5 27.1 %all-to-all-start.1 = ((bf16[16,304,128]{2,1,0:T(8,128)(2,1)}), bf16[16,304,128]{2,1,0:T(8,128)(2,1)S(1)}, u32[]{:S(2)}, u32[]{:S(2)}) async-start(bf16[16,304,128]{2,1,0:T(8,128)(2,1)} %copy-done.4), calls=%async_computation.1 | async-start | bytes 2490368 | tf_op jit(solution)/shard_map/all_to_all | solution.py:21
  30.3 20.4 %collective-permute-start = (bf16[256,128]{1,0:T(8,128)(2,1)}, bf16[256,128]{1,0:T(8,128)(2,1)S(1)}, u32[]{:S(2)}, u32[]{:S(2)}) collective-permute-start(bf16[256,128]{1,0:T(8,128)(2,1)} %get-tuple-element.17), channel_id=1, source_target_pairs={{0,0},{1,1},{2,2},{3,3},{4,4},{5,5},{6,6},{7,7},{8,64},{9,65},{10,... | collective-permute-start | bytes 196616 | tf_op jit(solution)/shard_map/ppermute | solution.py:34
  60.2 1.3 copy-start.1
  61.6 6.9 %copy-start.7 = (f32[2,64,128]{2,1,0:T(8,128)S(1)}, f32[2,64,128]{2,1,0:T(8,128)}, u32[]{:S(2)}) copy-start(f32[2,64,128]{2,1,0:T(8,128)} %param.5) | copy-start | bytes 196612
  61.6 37.3 %all-to-all-start.3 = ((bf16[16,512,128]{2,1,0:T(8,128)(2,1)}), bf16[16,512,128]{2,1,0:T(8,128)(2,1)}, u32[]{:S(2)}, u32[]{:S(2)}) async-start(bf16[16,512,128]{2,1,0:T(8,128)(2,1)} %copy-done.1), calls=%async_computation.3 | async-start | bytes 4194304 | tf_op jit(solution)/shard_map/all_to_all | solution.py:21
  68.4 68.9 %all-gather.3.cloned.1.call-start = ((), (), s32[]{:S(2)}) async-start(), calls=%async_computation.6 | async-start | bytes 1179648 | tf_op jit(solution)/shard_map/all_gather | solution.py:231
  69.1 29.7 %collective-permute-start.1 = (bf16[256,128]{1,0:T(8,128)(2,1)S(1)}, bf16[256,128]{1,0:T(8,128)(2,1)S(1)}, u32[]{:S(2)}, u32[]{:S(2)}) collective-permute-start(bf16[256,128]{1,0:T(8,128)(2,1)S(1)} %get-tuple-element.21), channel_id=1, source_target_pairs={{0,0},{1,1},{2,2},{3,3},{4,4},{5,5},{6,6},{7,7},{8,64},{9,65},{10,... | collective-permute-start | bytes 196616 | tf_op jit(solution)/shard_map/ppermute | solution.py:34
  122.2 27.2 %all-to-all-start.5 = ((f32[32,2,128]{2,1,0:T(2,128)}), f32[32,2,128]{2,1,0:T(2,128)S(1)}, u32[]{:S(2)}, u32[]{:S(2)}) async-start(f32[32,2,128]{2,1,0:T(2,128)} %sums.1), calls=%async_computation.5 | async-start | bytes 65536 | tf_op jit(solution)/shard_map/all_to_all | solution.py:21
  137.3 1.2 copy-start.5
  141.2 1.3 copy-start.2
  149.4 1.6 copy-start.3
Sparse Core Ops, SparseCore 0:
  72.0 51.7 all-gather.2

commit v4 on v3

--- a/solution.py
+++ b/solution.py
@@ -174,32 +174,32 @@
         jnp.sum(forward[...] * prop, axis=1, keepdims=True),
         jnp.sum(prop, axis=1, keepdims=True),
     )
-    pieces = [piece.astype(F32) for piece in split3(rows)]
-    tail = jnp.concatenate(pieces + [jnp.zeros((8, 128), F32)], axis=0).astype(BF)
+    pieces = [piece.astype(F32)[0:4] for piece in split3(rows)]
+    tail = jnp.concatenate(pieces + [jnp.zeros((4, 128), F32)], axis=0).astype(BF)
     for p in range(PLANES):
         out[p, 0:256, :] = far[...]
-        out[p, 256:288, :] = tail
+        out[p, 256:272, :] = tail
 
 
 def sum_body(got, out):
-    total = jnp.zeros((32, 128), F32)
-    for p in range(PLANES):
-        total += got[p, 256:288, :].astype(F32)
-    total = total[0:8] + total[8:16] + total[16:24]
+    total = jnp.zeros((16, 128), F32)
+    for p in range(PLANES):
+        total += got[p, 256:272, :].astype(F32)
+    total = total[0:4] + total[4:8] + total[8:12]
     both = total[0:1] + pltpu.roll(total[1:2], 64, axis=1)
     pair = jnp.concatenate([both, total[2:3]], axis=0)
     for k in range(GROUPS * LINES):
         out[k] = pair
 
 
-def prepare_body(late, early, forward, right, held, sems):
+def prepare_body(late, early, forward, right1, right0, held, sems):
     copies = []
     for g in range(GROUPS):
         copies.append(pltpu.make_async_copy(forward.at[g, pl.ds(0, 2)], held.at[g], sems.at[g]))
         copies[-1].start()
-    for t, (src, first) in enumerate(((late, 256), (early, 0))):
+    for src, first, right in ((late, 256, right1), (early, 0, right0)):
         for g in range(GROUPS):
-            at = t * 512 + g * 64
+            at = g * 64
             for c in range(GROUPS):
                 rows = first + c % LINES * 64
                 right[at : at + 64, c * 128 : (c + 1) * 128] = src[
@@ -209,7 +209,7 @@
         copy.wait()
 
 
-def count_body(width, group, got, forward, prop, right, backward, count, left):
+def count_body(width, group, got, forward, prop, right1, right0, backward, count, left):
     def columns(first):
         pair = jnp.sum(got[pl.ds(first, LINES)], axis=0) / width
         table = jnp.concatenate([pair, jnp.zeros((6, 128), F32)], axis=0).T
@@ -221,7 +221,9 @@
         for t in range(2):
             at = t * 512 + g * 64
             left[at : at + 64, :] = (forward[g, 1 - t] / post[t]).astype(BF)
-    count[...] = jnp.dot(left[...].T, right[...], preferred_element_type=F32) * (1.0 / 1024)
+    total = jnp.dot(left[0:512, :].T, right1[...], preferred_element_type=F32)
+    total += jnp.dot(left[512:1024, :].T, right0[...], preferred_element_type=F32)
+    count[...] = total * (1.0 / 1024)
 
 
 def on_device(forward_probs, backward_last, emission, token_ids, transition):
@@ -279,16 +281,16 @@
         second_body,
         [("vmem", got), ("vmem", transition), ("vmem", forward_probs[0]), ("vmem", post1)]
         + [("vmem", far0)],
-        [((64, 128), F32, "vmem"), ((16, 288, 128), BF, "vmem")],
+        [((64, 128), F32, "vmem"), ((16, 272, 128), BF, "vmem")],
         [wide],
     )
     early = exchange(sent, PLANE)
     (sent,) = call("sums", sum_body, [("vmem", early)], [((32, 2, 128), F32, "vmem")])
-    right, forward = call(
+    right1, right0, forward = call(
         "prepare",
         prepare_body,
         [("vmem", got), ("vmem", early), ("any", forward_all)],
-        [((1024, 1024), BF, "vmem"), ((8, 2, 64, 128), F32, "vmem")],
+        [((512, 1024), BF, "vmem")] * 2 + [((8, 2, 64, 128), F32, "vmem")],
         [pltpu.SemaphoreType.DMA((GROUPS,))],
     )
     got = exchange(sent, LINE)
@@ -297,7 +299,8 @@
         call(
             "counts",
             functools.partial(count_body, width),
-            [("smem", group), ("vmem", got), ("vmem", forward), ("vmem", prop0), ("vmem", right)],
+            [("smem", group), ("vmem", got), ("vmem", forward), ("vmem", prop0)]
+            + [("vmem", right1), ("vmem", right0)],
             [((64, 128), F32, "vmem"), ((128, 1024), F32, "vmem")],
             [pltpu.VMEM((1024, 128), BF)],
         )

time: 160 us -> 159 us (level)
  no operation moved by 1% of the time
where the time goes in v4:
time: 159 us; the launch traced here: 158 us
  starting transfers between devices  45.2 us (28%)
  waiting for transfers between devices  40.1 us (25%)
  blocking collectives  38.8 us (24%)
  between operations  14.2 us (9%)
  Pallas kernels  13.1 us (8%)
  local copies, waits for them, and re-layouts  6.2 us (4%)
    all_to_all x3, blocking collectives, exchange(): return lax.all_to_all(blocks, axes, 0, 0, tiled=True)  38.8 us
    ppermute x2, waiting for transfers between devices, swap_groups(): return lax.ppermute(block, AXES, pairs)  32.7 us
    all_to_all x3, starting transfers between devices, exchange(): return lax.all_to_all(blocks, axes, 0, 0, tiled=True)  28.7 us
    ppermute x2, starting transfers between devices, swap_groups(): return lax.ppermute(block, AXES, pairs)  16.5 us
    pallas_call x8, Pallas kernels, call(): pl.pallas_call(kernel, out_shape=[jax.ShapeDtypeStruct(s, d) for s, d, _...  13.1 us
    all_to_all x3, waiting for transfers between devices, exchange(): return lax.all_to_all(blocks, axes, 0, 0, tiled=True)  7.36 us
    unnamed x16, local copies, waits for them, and re-layouts  5.42 us
  transfers between devices with their start and end apart: 6, of which 3 were waited for; matrix products, arithmetic and copies ran while one was open for 1% of the time, Pallas kernels for 4%

profile of v4, /device:TPU:1, one launch (start us, length us, event | category | flops | bytes accessed | tf_op | source)
XLA Modules:
  0.0 158.2 jit_solution(14012736971738455484)
XLA Ops:
  7.2 3.2 %start.1 = (bf16[4,112,128]{2,1,0:T(8,128)(2,1)}, f32[64,128]{1,0:T(8,128)}) custom-call(s32[2,64]{1,0:T(2,128)} %bitcast.9, f32[1024,128]{1,0:T(8,128)} %refs_1_.2, f32[64,128]{1,0:T(8,128)} %refs_2_.2, bf16[128,8192]{1,0:T(8,128)(2,1)} %refs_1_.3), custom_call_target="tpu_custom_call" | custom-call | tf_op jit(solution)/shard_map/start/pallas_call | solution.py:49
  10.4 11.2 %all_to_all.30.refs_0_ = bf16[4,112,128]{2,1,0:T(8,128)(2,1)S(1)} all-to-all(bf16[4,112,128]{2,1,0:T(8,128)(2,1)} %get-tuple-element.15), channel_id=1, replica_groups=mesh['zh'=4,'co'=2,'y'=4,'xh'=2,'xl'=2,'zl'=4] {'zl'}, dimensions={0} | all-to-all | bytes 229376 | tf_op jit(solution)/shard_map/all_to_all | solution.py:21
  21.5 0.8 line.1
  22.3 1.1 copy-done.2
  23.4 6.9 %all-to-all-start.1 = ((bf16[16,304,128]{2,1,0:T(8,128)(2,1)}), bf16[16,304,128]{2,1,0:T(8,128)(2,1)S(1)}, u32[]{:S(2)}, u32[]{:S(2)}) async-start(bf16[16,304,128]{2,1,0:T(8,128)(2,1)} %copy-done.2), calls=%async_computation.1 | async-start | bytes 2490368 | tf_op jit(solution)/shard_map/all_to_all | solution.py:21
  30.3 7.3 %collective-permute-start = (bf16[256,128]{1,0:T(8,128)(2,1)}, bf16[256,128]{1,0:T(8,128)(2,1)S(1)}, u32[]{:S(2)}, u32[]{:S(2)}) collective-permute-start(bf16[256,128]{1,0:T(8,128)(2,1)} %get-tuple-element.18), channel_id=1, source_target_pairs={{0,0},{1,1},{2,2},{3,3},{4,4},{5,5},{6,6},{7,7},{8,64},{9,65},{10,... | collective-permute-start | bytes 196616 | tf_op jit(solution)/shard_map/ppermute | solution.py:34
  37.6 0.8 slice_bitcast_fusion
  38.4 12.2 %collective-permute-done.refs_5_.refs_1_ = bf16[256,128]{1,0:T(8,128)(2,1)S(1)} collective-permute-done((bf16[256,128]{1,0:T(8,128)(2,1)}, bf16[256,128]{1,0:T(8,128)(2,1)S(1)}, u32[]{:S(2)}, u32[]{:S(2)}) %collective-permute-start) | collective-permute-done | bytes 65568 | tf_op jit(solution)/shard_map/ppermute | solution.py:34
  50.6 0.0 all-to-all-done.1.refs_1_
  50.7 1.0 first.1
  51.6 8.2 %all_to_all.31.refs_0_ = f32[4,72,128]{2,1,0:T(8,128)S(1)} all-to-all(f32[4,72,128]{2,1,0:T(8,128)S(1)} %get-tuple-element.19), channel_id=1, replica_groups=mesh['zh'=4,'co'=2,'y'=4,'xh'=2,'xl'=2,'zl'=4] {'zl'}, dimensions={0} | all-to-all | bytes 294912 | tf_op jit(solution)/shard_map/all_to_all | solution.py:21
  59.8 0.4 round.1
  60.2 1.3 copy-done.1
  61.5 6.8 %all-to-all-start.3 = ((bf16[16,512,128]{2,1,0:T(8,128)(2,1)}), bf16[16,512,128]{2,1,0:T(8,128)(2,1)}, u32[]{:S(2)}, u32[]{:S(2)}) async-start(bf16[16,512,128]{2,1,0:T(8,128)(2,1)} %copy-done.1), calls=%async_computation.3 | async-start | bytes 4194304 | tf_op jit(solution)/shard_map/all_to_all | solution.py:21
  68.4 0.0 all-gather.3.cloned.1.call-start
  68.4 0.7 pad_maximum_fusion
  69.1 0.0 all-gather.3.cloned.1.call-update
  69.1 9.2 %collective-permute-start.1 = (bf16[256,128]{1,0:T(8,128)(2,1)S(1)}, bf16[256,128]{1,0:T(8,128)(2,1)S(1)}, u32[]{:S(2)}, u32[]{:S(2)}) collective-permute-start(bf16[256,128]{1,0:T(8,128)(2,1)S(1)} %get-tuple-element.22), channel_id=1, source_target_pairs={{0,0},{1,1},{2,2},{3,3},{4,4},{5,5},{6,6},{7,7},{8,64},{9,65},{10,... | collective-permute-start | bytes 196616 | tf_op jit(solution)/shard_map/ppermute | solution.py:34
  78.3 20.5 %collective-permute-done.1.refs_4_ = bf16[256,128]{1,0:T(8,128)(2,1)S(1)} collective-permute-done((bf16[256,128]{1,0:T(8,128)(2,1)S(1)}, bf16[256,128]{1,0:T(8,128)(2,1)S(1)}, u32[]{:S(2)}, u32[]{:S(2)}) %collective-permute-start.1) | collective-permute-done | bytes 65568 | tf_op jit(solution)/shard_map/ppermute | solution.py:34
  98.8 0.0 all-to-all-done.3.refs_0_
  98.8 2.7 %second.1 = (f32[64,128]{1,0:T(8,128)S(1)}, bf16[16,272,128]{2,1,0:T(8,128)(2,1)S(1)}) custom-call(bf16[16,512,128]{2,1,0:T(8,128)(2,1)} %all-to-all-done.3.refs_0_, bf16[128,8192]{1,0:T(8,128)(2,1)S(1)} %copy-done, f32[64,128]{1,0:T(8,128)S(1)} %get-tuple-element.28.refs_2_, f32[64,128]{1,0:T(8,128)S(1)} %get-tuple-element.21.refs_3_, ...), custom_call_target="tpu_custom_call" | custom-call | tf_op jit(solution)/shard_map/second/pallas_call | solution.py:49
  101.5 19.4 %all_to_all.32.refs_0_.refs_1_ = bf16[16,272,128]{2,1,0:T(8,128)(2,1)S(1)} all-to-all(bf16[16,272,128]{2,1,0:T(8,128)(2,1)S(1)} %get-tuple-element.23), channel_id=1, replica_groups=mesh['zh'=4,'co'=2,'y'=4,'xh'=2,'xl'=2,'zl'=4] {'y','xh','xl'}, dimensions={0} | all-to-all | bytes 2228224 | tf_op jit(solution)/shard_map/all_to_all | solution.py:21
  120.9 0.7 sums.1
  121.6 14.9 %all-to-all-start.5 = ((f32[32,2,128]{2,1,0:T(2,128)}), f32[32,2,128]{2,1,0:T(2,128)S(1)}, u32[]{:S(2)}, u32[]{:S(2)}) async-start(f32[32,2,128]{2,1,0:T(2,128)} %sums.1), calls=%async_computation.5 | async-start | bytes 65536 | tf_op jit(solution)/shard_map/all_to_all | solution.py:21
  136.6 0.0 all-gather.3.cloned.1.call-done
  136.6 1.2 copy-done.3
  137.9 2.7 %prepare.1 = (bf16[512,1024]{1,0:T(8,128)(2,1)S(1)}, bf16[512,1024]{1,0:T(8,128)(2,1)S(1)}, f32[8,2,64,128]{3,2,1,0:T(8,128)S(1)}) custom-call(bf16[16,512,128]{2,1,0:T(8,128)(2,1)} %all-to-all-done.3.refs_0_, bf16[16,272,128]{2,1,0:T(8,128)(2,1)S(1)} %all_to_all.32.refs_0_.refs_1_, f32[8,4,64,128]{3,2,1,0:T(8,128)S(1)} %bitcast.8), custom_call_target="tpu_custom_call" | custom-call | tf_op jit(solution)/shard_map/prepare/pallas_call | solution.py:49
  140.6 0.0 copy-start.4
  140.6 0.8 copy-done.4
  141.3 7.4 %all-to-all-done.5.refs_1_ = f32[32,2,128]{2,1,0:T(2,128)S(1)} async-done(((f32[32,2,128]{2,1,0:T(2,128)}), f32[32,2,128]{2,1,0:T(2,128)S(1)}, u32[]{:S(2)}, u32[]{:S(2)}) %all-to-all-start.5) | async-done | bytes 32800 | tf_op jit(solution)/shard_map/all_to_all | solution.py:21
  148.7 1.0 copy-done.5
  149.7 1.7 %counts.1 = (f32[64,128]{1,0:T(8,128)}, f32[128,1024]{1,0:T(8,128)}) custom-call(s32[1]{0:T(128)} %bitcast.refs_0_, f32[32,2,128]{2,1,0:T(2,128)S(1)} %all-to-all-done.5.refs_1_, f32[8,2,64,128]{3,2,1,0:T(8,128)S(1)} %copy-done.5, f32[64,128]{1,0:T(8,128)S(1)} %get-tuple-element.25.refs_3_, bf16[512,1024]{1,0:T(8,128)(2,1)S(1)} %get-tuple-element.26.refs_4_, ...), custom_call_target="tpu_custom_call" | custom-call | tf_op jit(solution)/shard_map/counts/pallas_call | solution.py:49
  (10 shorter events, 0.0 us)
Async XLA Ops:
  22.3 1.1 copy-start.2
  23.4 27.3 %copy-start = (bf16[128,8192]{1,0:T(8,128)(2,1)S(1)}, bf16[128,8192]{1,0:T(8,128)(2,1)}, u32[]{:S(2)}) copy-start(bf16[128,8192]{1,0:T(8,128)(2,1)} %refs_1_.3) | copy-start | bytes 6291460
  23.4 27.3 %copy-start.6 = (f32[64,128]{1,0:T(8,128)S(1)}, f32[64,128]{1,0:T(8,128)}, u32[]{:S(2)}) copy-start(f32[64,128]{1,0:T(8,128)} %get-tuple-element.17.refs_3_) | copy-start | bytes 98308
  23.4 27.3 %all-to-all-start.1 = ((bf16[16,304,128]{2,1,0:T(8,128)(2,1)}), bf16[16,304,128]{2,1,0:T(8,128)(2,1)S(1)}, u32[]{:S(2)}, u32[]{:S(2)}) async-start(bf16[16,304,128]{2,1,0:T(8,128)(2,1)} %copy-done.2), calls=%async_computation.1 | async-start | bytes 2490368 | tf_op jit(solution)/shard_map/all_to_all | solution.py:21
  30.3 20.4 %collective-permute-start = (bf16[256,128]{1,0:T(8,128)(2,1)}, bf16[256,128]{1,0:T(8,128)(2,1)S(1)}, u32[]{:S(2)}, u32[]{:S(2)}) collective-permute-start(bf16[256,128]{1,0:T(8,128)(2,1)} %get-tuple-element.18), channel_id=1, source_target_pairs={{0,0},{1,1},{2,2},{3,3},{4,4},{5,5},{6,6},{7,7},{8,64},{9,65},{10,... | collective-permute-start | bytes 196616 | tf_op jit(solution)/shard_map/ppermute | solution.py:34
  60.2 1.3 copy-start.1
  61.5 6.9 %copy-start.7 = (f32[2,64,128]{2,1,0:T(8,128)S(1)}, f32[2,64,128]{2,1,0:T(8,128)}, u32[]{:S(2)}) copy-start(f32[2,64,128]{2,1,0:T(8,128)} %param.5) | copy-start | bytes 196612
  61.5 37.3 %all-to-all-start.3 = ((bf16[16,512,128]{2,1,0:T(8,128)(2,1)}), bf16[16,512,128]{2,1,0:T(8,128)(2,1)}, u32[]{:S(2)}, u32[]{:S(2)}) async-start(bf16[16,512,128]{2,1,0:T(8,128)(2,1)} %copy-done.1), calls=%async_computation.3 | async-start | bytes 4194304 | tf_op jit(solution)/shard_map/all_to_all | solution.py:21
  68.4 68.2 %all-gather.3.cloned.1.call-start = ((), (), s32[]{:S(2)}) async-start(), calls=%async_computation.6 | async-start | bytes 1179648 | tf_op jit(solution)/shard_map/all_gather | solution.py:233
  69.1 29.7 %collective-permute-start.1 = (bf16[256,128]{1,0:T(8,128)(2,1)S(1)}, bf16[256,128]{1,0:T(8,128)(2,1)S(1)}, u32[]{:S(2)}, u32[]{:S(2)}) collective-permute-start(bf16[256,128]{1,0:T(8,128)(2,1)S(1)} %get-tuple-element.22), channel_id=1, source_target_pairs={{0,0},{1,1},{2,2},{3,3},{4,4},{5,5},{6,6},{7,7},{8,64},{9,65},{10,... | collective-permute-start | bytes 196616 | tf_op jit(solution)/shard_map/ppermute | solution.py:34
  121.6 27.1 %all-to-all-start.5 = ((f32[32,2,128]{2,1,0:T(2,128)}), f32[32,2,128]{2,1,0:T(2,128)S(1)}, u32[]{:S(2)}, u32[]{:S(2)}) async-start(f32[32,2,128]{2,1,0:T(2,128)} %sums.1), calls=%async_computation.5 | async-start | bytes 65536 | tf_op jit(solution)/shard_map/all_to_all | solution.py:21
  136.6 1.2 copy-start.3
  140.6 0.8 copy-start.4
  148.7 1.0 copy-start.5
Sparse Core Ops, SparseCore 0:
  71.9 51.7 all-gather.2

commit v5 on v4

--- a/solution.py
+++ b/solution.py
@@ -166,8 +166,19 @@
         out[p, 256:512, :] = far[...]
 
 
-def second_body(got, trans, forward, post, far, prop_out, out, wide):
-    prop = propagate(got, trans, wide)
+def second_body(got, trans, forward, post, far, prop_out, out, wide, rows, sems):
+    copies = []
+    for k in range(4):
+        part = pl.ds(k * 4, 4)
+        copies.append(
+            pltpu.make_async_copy(got.at[part, pl.ds(0, 256)], rows.at[part], sems.at[k])
+        )
+        copies[-1].start()
+    for p in range(PLANES):
+        out[p, 0:256, :] = far[...]
+    for copy in copies:
+        copy.wait()
+    prop = propagate(rows, trans, wide)
     prop_out[...] = prop
     rows = to_rows(
         post[:, 0:1],
@@ -177,7 +188,6 @@
     pieces = [piece.astype(F32)[0:4] for piece in split3(rows)]
     tail = jnp.concatenate(pieces + [jnp.zeros((4, 128), F32)], axis=0).astype(BF)
     for p in range(PLANES):
-        out[p, 0:256, :] = far[...]
         out[p, 256:272, :] = tail
 
 
@@ -279,10 +289,10 @@
     prop0, sent = call(
         "second",
         second_body,
-        [("vmem", got), ("vmem", transition), ("vmem", forward_probs[0]), ("vmem", post1)]
+        [("any", got), ("vmem", transition), ("vmem", forward_probs[0]), ("vmem", post1)]
         + [("vmem", far0)],
         [((64, 128), F32, "vmem"), ((16, 272, 128), BF, "vmem")],
-        [wide],
+        [wide, pltpu.VMEM((16, 256, 128), BF), pltpu.SemaphoreType.DMA((4,))],
     )
     early = exchange(sent, PLANE)
     (sent,) = call("sums", sum_body, [("vmem", early)], [((32, 2, 128), F32, "vmem")])

time: 159 us -> 159 us (level)
  no operation moved by 1% of the time
where the time goes in v5:
time: 159 us; the launch traced here: 158 us
  starting transfers between devices  45.2 us (28%)
  waiting for transfers between devices  40.1 us (25%)
  blocking collectives  38.8 us (24%)
  between operations  14.2 us (9%)
  Pallas kernels  12.6 us (8%)
  local copies, waits for them, and re-layouts  6.2 us (4%)
    all_to_all x3, blocking collectives, exchange(): return lax.all_to_all(blocks, axes, 0, 0, tiled=True)  38.8 us
    ppermute x2, waiting for transfers between devices, swap_groups(): return lax.ppermute(block, AXES, pairs)  32.7 us
    all_to_all x3, starting transfers between devices, exchange(): return lax.all_to_all(blocks, axes, 0, 0, tiled=True)  28.7 us
    ppermute x2, starting transfers between devices, swap_groups(): return lax.ppermute(block, AXES, pairs)  16.5 us
    pallas_call x8, Pallas kernels, call(): pl.pallas_call(kernel, out_shape=[jax.ShapeDtypeStruct(s, d) for s, d, _...  12.6 us
    all_to_all x3, waiting for transfers between devices, exchange(): return lax.all_to_all(blocks, axes, 0, 0, tiled=True)  7.36 us
    unnamed x16, local copies, waits for them, and re-layouts  5.42 us
  transfers between devices with their start and end apart: 6, of which 3 were waited for; matrix products, arithmetic and copies ran while one was open for 1% of the time, Pallas kernels for 4%

profile of v5, /device:TPU:1, one launch (start us, length us, event | category | flops | bytes accessed | tf_op | source)
XLA Modules:
  0.0 157.8 jit_solution(51027414984562368)
XLA Ops:
  7.2 3.2 %start.1 = (bf16[4,112,128]{2,1,0:T(8,128)(2,1)}, f32[64,128]{1,0:T(8,128)}) custom-call(s32[2,64]{1,0:T(2,128)} %bitcast.9, f32[1024,128]{1,0:T(8,128)} %refs_1_.2, f32[64,128]{1,0:T(8,128)} %refs_2_.2, bf16[128,8192]{1,0:T(8,128)(2,1)} %refs_1_.3), custom_call_target="tpu_custom_call" | custom-call | tf_op jit(solution)/shard_map/start/pallas_call | solution.py:49
  10.4 11.2 %all_to_all.30.refs_0_ = bf16[4,112,128]{2,1,0:T(8,128)(2,1)S(1)} all-to-all(bf16[4,112,128]{2,1,0:T(8,128)(2,1)} %get-tuple-element.15), channel_id=1, replica_groups=mesh['zh'=4,'co'=2,'y'=4,'xh'=2,'xl'=2,'zl'=4] {'zl'}, dimensions={0} | all-to-all | bytes 229376 | tf_op jit(solution)/shard_map/all_to_all | solution.py:21
  21.5 0.8 line.1
  22.3 1.1 copy-done.2
  23.4 6.9 %all-to-all-start.1 = ((bf16[16,304,128]{2,1,0:T(8,128)(2,1)}), bf16[16,304,128]{2,1,0:T(8,128)(2,1)S(1)}, u32[]{:S(2)}, u32[]{:S(2)}) async-start(bf16[16,304,128]{2,1,0:T(8,128)(2,1)} %copy-done.2), calls=%async_computation.1 | async-start | bytes 2490368 | tf_op jit(solution)/shard_map/all_to_all | solution.py:21
  30.3 7.3 %collective-permute-start = (bf16[256,128]{1,0:T(8,128)(2,1)}, bf16[256,128]{1,0:T(8,128)(2,1)S(1)}, u32[]{:S(2)}, u32[]{:S(2)}) collective-permute-start(bf16[256,128]{1,0:T(8,128)(2,1)} %get-tuple-element.18), channel_id=1, source_target_pairs={{0,0},{1,1},{2,2},{3,3},{4,4},{5,5},{6,6},{7,7},{8,64},{9,65},{10,... | collective-permute-start | bytes 196616 | tf_op jit(solution)/shard_map/ppermute | solution.py:34
  37.6 0.8 slice_bitcast_fusion
  38.4 12.2 %collective-permute-done.refs_5_.refs_1_ = bf16[256,128]{1,0:T(8,128)(2,1)S(1)} collective-permute-done((bf16[256,128]{1,0:T(8,128)(2,1)}, bf16[256,128]{1,0:T(8,128)(2,1)S(1)}, u32[]{:S(2)}, u32[]{:S(2)}) %collective-permute-start) | collective-permute-done | bytes 65568 | tf_op jit(solution)/shard_map/ppermute | solution.py:34
  50.6 0.0 all-to-all-done.1.refs_1_
  50.7 1.0 first.1
  51.6 8.2 %all_to_all.31.refs_0_ = f32[4,72,128]{2,1,0:T(8,128)S(1)} all-to-all(f32[4,72,128]{2,1,0:T(8,128)S(1)} %get-tuple-element.19), channel_id=1, replica_groups=mesh['zh'=4,'co'=2,'y'=4,'xh'=2,'xl'=2,'zl'=4] {'zl'}, dimensions={0} | all-to-all | bytes 294912 | tf_op jit(solution)/shard_map/all_to_all | solution.py:21
  59.8 0.4 round.1
  60.2 1.3 copy-done.1
  61.5 6.8 %all-to-all-start.3 = ((bf16[16,512,128]{2,1,0:T(8,128)(2,1)}), bf16[16,512,128]{2,1,0:T(8,128)(2,1)}, u32[]{:S(2)}, u32[]{:S(2)}) async-start(bf16[16,512,128]{2,1,0:T(8,128)(2,1)} %copy-done.1), calls=%async_computation.3 | async-start | bytes 4194304 | tf_op jit(solution)/shard_map/all_to_all | solution.py:21
  68.4 0.0 all-gather.3.cloned.1.call-start
  68.4 0.7 pad_maximum_fusion
  69.1 0.0 all-gather.3.cloned.1.call-update
  69.1 9.2 %collective-permute-start.1 = (bf16[256,128]{1,0:T(8,128)(2,1)S(1)}, bf16[256,128]{1,0:T(8,128)(2,1)S(1)}, u32[]{:S(2)}, u32[]{:S(2)}) collective-permute-start(bf16[256,128]{1,0:T(8,128)(2,1)S(1)} %get-tuple-element.22), channel_id=1, source_target_pairs={{0,0},{1,1},{2,2},{3,3},{4,4},{5,5},{6,6},{7,7},{8,64},{9,65},{10,... | collective-permute-start | bytes 196616 | tf_op jit(solution)/shard_map/ppermute | solution.py:34
  78.3 20.5 %collective-permute-done.1.refs_4_ = bf16[256,128]{1,0:T(8,128)(2,1)S(1)} collective-permute-done((bf16[256,128]{1,0:T(8,128)(2,1)S(1)}, bf16[256,128]{1,0:T(8,128)(2,1)S(1)}, u32[]{:S(2)}, u32[]{:S(2)}) %collective-permute-start.1) | collective-permute-done | bytes 65568 | tf_op jit(solution)/shard_map/ppermute | solution.py:34
  98.8 0.0 all-to-all-done.3.refs_0_
  98.8 2.2 %second.1 = (f32[64,128]{1,0:T(8,128)S(1)}, bf16[16,272,128]{2,1,0:T(8,128)(2,1)S(1)}) custom-call(bf16[16,512,128]{2,1,0:T(8,128)(2,1)} %all-to-all-done.3.refs_0_, bf16[128,8192]{1,0:T(8,128)(2,1)S(1)} %copy-done, f32[64,128]{1,0:T(8,128)S(1)} %get-tuple-element.28.refs_2_, f32[64,128]{1,0:T(8,128)S(1)} %get-tuple-element.21.refs_3_, ...), custom_call_target="tpu_custom_call" | custom-call | tf_op jit(solution)/shard_map/second/pallas_call | solution.py:49
  101.0 19.4 %all_to_all.32.refs_0_.refs_1_ = bf16[16,272,128]{2,1,0:T(8,128)(2,1)S(1)} all-to-all(bf16[16,272,128]{2,1,0:T(8,128)(2,1)S(1)} %get-tuple-element.23), channel_id=1, replica_groups=mesh['zh'=4,'co'=2,'y'=4,'xh'=2,'xl'=2,'zl'=4] {'y','xh','xl'}, dimensions={0} | all-to-all | bytes 2228224 | tf_op jit(solution)/shard_map/all_to_all | solution.py:21
  120.5 0.7 sums.1
  121.2 14.9 %all-to-all-start.5 = ((f32[32,2,128]{2,1,0:T(2,128)}), f32[32,2,128]{2,1,0:T(2,128)S(1)}, u32[]{:S(2)}, u32[]{:S(2)}) async-start(f32[32,2,128]{2,1,0:T(2,128)} %sums.1), calls=%async_computation.5 | async-start | bytes 65536 | tf_op jit(solution)/shard_map/all_to_all | solution.py:21
  136.1 0.0 all-gather.3.cloned.1.call-done
  136.2 1.2 copy-done.3
  137.4 2.7 %prepare.1 = (bf16[512,1024]{1,0:T(8,128)(2,1)S(1)}, bf16[512,1024]{1,0:T(8,128)(2,1)S(1)}, f32[8,2,64,128]{3,2,1,0:T(8,128)S(1)}) custom-call(bf16[16,512,128]{2,1,0:T(8,128)(2,1)} %all-to-all-done.3.refs_0_, bf16[16,272,128]{2,1,0:T(8,128)(2,1)S(1)} %all_to_all.32.refs_0_.refs_1_, f32[8,4,64,128]{3,2,1,0:T(8,128)S(1)} %bitcast.8), custom_call_target="tpu_custom_call" | custom-call | tf_op jit(solution)/shard_map/prepare/pallas_call | solution.py:49
  140.1 0.0 copy-start.4
  140.1 0.8 copy-done.4
  140.9 7.4 %all-to-all-done.5.refs_1_ = f32[32,2,128]{2,1,0:T(2,128)S(1)} async-done(((f32[32,2,128]{2,1,0:T(2,128)}), f32[32,2,128]{2,1,0:T(2,128)S(1)}, u32[]{:S(2)}, u32[]{:S(2)}) %all-to-all-start.5) | async-done | bytes 32800 | tf_op jit(solution)/shard_map/all_to_all | solution.py:21
  148.2 1.0 copy-done.5
  149.3 1.7 %counts.1 = (f32[64,128]{1,0:T(8,128)}, f32[128,1024]{1,0:T(8,128)}) custom-call(s32[1]{0:T(128)} %bitcast.refs_0_, f32[32,2,128]{2,1,0:T(2,128)S(1)} %all-to-all-done.5.refs_1_, f32[8,2,64,128]{3,2,1,0:T(8,128)S(1)} %copy-done.5, f32[64,128]{1,0:T(8,128)S(1)} %get-tuple-element.25.refs_3_, bf16[512,1024]{1,0:T(8,128)(2,1)S(1)} %get-tuple-element.26.refs_4_, ...), custom_call_target="tpu_custom_call" | custom-call | tf_op jit(solution)/shard_map/counts/pallas_call | solution.py:49
  (10 shorter events, 0.0 us)
Async XLA Ops:
  22.3 1.1 copy-start.2
  23.4 27.3 %copy-start = (bf16[128,8192]{1,0:T(8,128)(2,1)S(1)}, bf16[128,8192]{1,0:T(8,128)(2,1)}, u32[]{:S(2)}) copy-start(bf16[128,8192]{1,0:T(8,128)(2,1)} %refs_1_.3) | copy-start | bytes 6291460
  23.4 27.3 %copy-start.6 = (f32[64,128]{1,0:T(8,128)S(1)}, f32[64,128]{1,0:T(8,128)}, u32[]{:S(2)}) copy-start(f32[64,128]{1,0:T(8,128)} %get-tuple-element.17.refs_3_) | copy-start | bytes 98308
  23.4 27.3 %all-to-all-start.1 = ((bf16[16,304,128]{2,1,0:T(8,128)(2,1)}), bf16[16,304,128]{2,1,0:T(8,128)(2,1)S(1)}, u32[]{:S(2)}, u32[]{:S(2)}) async-start(bf16[16,304,128]{2,1,0:T(8,128)(2,1)} %copy-done.2), calls=%async_computation.1 | async-start | bytes 2490368 | tf_op jit(solution)/shard_map/all_to_all | solution.py:21
  30.3 20.4 %collective-permute-start = (bf16[256,128]{1,0:T(8,128)(2,1)}, bf16[256,128]{1,0:T(8,128)(2,1)S(1)}, u32[]{:S(2)}, u32[]{:S(2)}) collective-permute-start(bf16[256,128]{1,0:T(8,128)(2,1)} %get-tuple-element.18), channel_id=1, source_target_pairs={{0,0},{1,1},{2,2},{3,3},{4,4},{5,5},{6,6},{7,7},{8,64},{9,65},{10,... | collective-permute-start | bytes 196616 | tf_op jit(solution)/shard_map/ppermute | solution.py:34
  60.2 1.3 copy-start.1
  61.5 6.9 %copy-start.7 = (f32[2,64,128]{2,1,0:T(8,128)S(1)}, f32[2,64,128]{2,1,0:T(8,128)}, u32[]{:S(2)}) copy-start(f32[2,64,128]{2,1,0:T(8,128)} %param.5) | copy-start | bytes 196612
  61.5 37.3 %all-to-all-start.3 = ((bf16[16,512,128]{2,1,0:T(8,128)(2,1)}), bf16[16,512,128]{2,1,0:T(8,128)(2,1)}, u32[]{:S(2)}, u32[]{:S(2)}) async-start(bf16[16,512,128]{2,1,0:T(8,128)(2,1)} %copy-done.1), calls=%async_computation.3 | async-start | bytes 4194304 | tf_op jit(solution)/shard_map/all_to_all | solution.py:21
  68.4 67.8 %all-gather.3.cloned.1.call-start = ((), (), s32[]{:S(2)}) async-start(), calls=%async_computation.6 | async-start | bytes 1179648 | tf_op jit(solution)/shard_map/all_gather | solution.py:243
  69.1 29.7 %collective-permute-start.1 = (bf16[256,128]{1,0:T(8,128)(2,1)S(1)}, bf16[256,128]{1,0:T(8,128)(2,1)S(1)}, u32[]{:S(2)}, u32[]{:S(2)}) collective-permute-start(bf16[256,128]{1,0:T(8,128)(2,1)S(1)} %get-tuple-element.22), channel_id=1, source_target_pairs={{0,0},{1,1},{2,2},{3,3},{4,4},{5,5},{6,6},{7,7},{8,64},{9,65},{10,... | collective-permute-start | bytes 196616 | tf_op jit(solution)/shard_map/ppermute | solution.py:34
  121.2 27.1 %all-to-all-start.5 = ((f32[32,2,128]{2,1,0:T(2,128)}), f32[32,2,128]{2,1,0:T(2,128)S(1)}, u32[]{:S(2)}, u32[]{:S(2)}) async-start(f32[32,2,128]{2,1,0:T(2,128)} %sums.1), calls=%async_computation.5 | async-start | bytes 65536 | tf_op jit(solution)/shard_map/all_to_all | solution.py:21
  136.2 1.2 copy-start.3
  140.1 0.8 copy-start.4
  148.2 1.0 copy-start.5
Sparse Core Ops, SparseCore 0:
  71.9 51.7 all-gather.2

commit v6 on v5

--- a/solution.py
+++ b/solution.py
@@ -145,13 +145,16 @@
         scale += got[p, pl.ds(own, 64), :].astype(F32) * sums[p : p + 1, :]
     scale = jnp.sum(scale, axis=1, keepdims=True)
     peak = jnp.max(prop, axis=1, keepdims=True)
-    value, info = emitted[...] * (prop / peak), to_rows(peak, scale)
-    for k in range(LINES):
-        out[k, 0:64, :] = value
-        out[k, 64:72, :] = info
+    out[0:64, :] = emitted[...] * (prop / peak)
+    out[64:72, :] = to_rows(peak, scale)
     post[...] = jnp.broadcast_to(
         jnp.sum(forward[...] * prop, axis=1, keepdims=True), (64, 128)
     )
+
+
+def repeat_body(got, out):
+    for k in range(LINES):
+        out[k] = got[...]
 
 
 def round_body(width, got, far, line, out):
@@ -273,8 +276,15 @@
             ("vmem", emitted),
             ("vmem", forward_probs[1]),
         ],
-        [((4, 72, 128), F32, "vmem"), ((64, 128), F32, "vmem")],
+        [((72, 128), F32, "vmem"), ((64, 128), F32, "vmem")],
         [wide],
+    )
+    (sent,) = call(
+        "repeat",
+        repeat_body,
+        [("vmem", sent)],
+        [((4, 72, 128), F32, "vmem")],
+        (),
         (far1,),
     )
     got = exchange(sent, "zl")

time: 159 us -> 159 us (level)
    ppermute x2, waiting for transfers between devices: 32.7 us -> 23 us  [swap_groups(): return lax.ppermute(block, AXES, pairs)]
    all_to_all x3, waiting for transfers between devices: 7.36 us -> 16 us  [exchange(): return lax.all_to_all(blocks, axes, 0, 0, tiled=True)]
    pallas_call x8 -> x9, Pallas kernels: 12.6 us -> 12.6 us  [call(): pl.pallas_call(kernel, out_shape=[jax.ShapeDtypeStruct(s, d) for s, d, _...]
  transfers between devices with their start and end apart: 6 -> 6, of which waited for: 3 -> 4; matrix products, arithmetic and copies ran while one was open for 1% -> 1% of each run, Pallas kernels for 4% -> 4%
where the time goes in v6:
time: 159 us; the launch traced here: 158 us
  starting transfers between devices  46.3 us (29%)
  waiting for transfers between devices  39.1 us (25%)
  blocking collectives  38.8 us (24%)
  between operations  14.2 us (9%)
  Pallas kernels  12.6 us (8%)
  local copies, waits for them, and re-layouts  6.2 us (4%)
    all_to_all x3, blocking collectives, exchange(): return lax.all_to_all(blocks, axes, 0, 0, tiled=True)  38.8 us
    all_to_all x3, starting transfers between devices, exchange(): return lax.all_to_all(blocks, axes, 0, 0, tiled=True)  29.8 us
    ppermute x2, waiting for transfers between devices, swap_groups(): return lax.ppermute(block, AXES, pairs)  23 us
    ppermute x2, starting transfers between devices, swap_groups(): return lax.ppermute(block, AXES, pairs)  16.5 us
    all_to_all x3, waiting for transfers between devices, exchange(): return lax.all_to_all(blocks, axes, 0, 0, tiled=True)  16 us
    pallas_call x9, Pallas kernels, call(): pl.pallas_call(kernel, out_shape=[jax.ShapeDtypeStruct(s, d) for s, d, _...  12.6 us
    unnamed x16, local copies, waits for them, and re-layouts  5.42 us
  transfers between devices with their start and end apart: 6, of which 4 were waited for; matrix products, arithmetic and copies ran while one was open for 1% of the time, Pallas kernels for 4%

profile of v6, /device:TPU:1, one launch (start us, length us, event | category | flops | bytes accessed | tf_op | source)
XLA Modules:
  0.0 157.9 jit_solution(18368439140640213195)
XLA Ops:
  7.2 3.2 %start.1 = (bf16[4,112,128]{2,1,0:T(8,128)(2,1)}, f32[64,128]{1,0:T(8,128)}) custom-call(s32[2,64]{1,0:T(2,128)} %bitcast.9, f32[1024,128]{1,0:T(8,128)} %refs_1_.2, f32[64,128]{1,0:T(8,128)} %refs_2_.2, bf16[128,8192]{1,0:T(8,128)(2,1)} %refs_1_.3), custom_call_target="tpu_custom_call" | custom-call | tf_op jit(solution)/shard_map/start/pallas_call | solution.py:49
  10.4 11.2 %all_to_all.30.refs_0_ = bf16[4,112,128]{2,1,0:T(8,128)(2,1)S(1)} all-to-all(bf16[4,112,128]{2,1,0:T(8,128)(2,1)} %get-tuple-element.15), channel_id=1, replica_groups=mesh['zh'=4,'co'=2,'y'=4,'xh'=2,'xl'=2,'zl'=4] {'zl'}, dimensions={0} | all-to-all | bytes 229376 | tf_op jit(solution)/shard_map/all_to_all | solution.py:21
  21.5 0.8 line.1
  22.3 1.1 copy-done.2
  23.4 6.9 %all-to-all-start.1 = ((bf16[16,304,128]{2,1,0:T(8,128)(2,1)}), bf16[16,304,128]{2,1,0:T(8,128)(2,1)S(1)}, u32[]{:S(2)}, u32[]{:S(2)}) async-start(bf16[16,304,128]{2,1,0:T(8,128)(2,1)} %copy-done.2), calls=%async_computation.1 | async-start | bytes 2490368 | tf_op jit(solution)/shard_map/all_to_all | solution.py:21
  30.3 7.3 %collective-permute-start = (bf16[256,128]{1,0:T(8,128)(2,1)}, bf16[256,128]{1,0:T(8,128)(2,1)S(1)}, u32[]{:S(2)}, u32[]{:S(2)}) collective-permute-start(bf16[256,128]{1,0:T(8,128)(2,1)} %get-tuple-element.19), channel_id=1, source_target_pairs={{0,0},{1,1},{2,2},{3,3},{4,4},{5,5},{6,6},{7,7},{8,64},{9,65},{10,... | collective-permute-start | bytes 196616 | tf_op jit(solution)/shard_map/ppermute | solution.py:34
  37.6 0.8 slice_bitcast_fusion
  38.4 8.7 %all-to-all-done.1.refs_1_ = bf16[16,304,128]{2,1,0:T(8,128)(2,1)S(1)} async-done(((bf16[16,304,128]{2,1,0:T(8,128)(2,1)}), bf16[16,304,128]{2,1,0:T(8,128)(2,1)S(1)}, u32[]{:S(2)}, u32[]{:S(2)}) %all-to-all-start.1) | async-done | bytes 1245216 | tf_op jit(solution)/shard_map/all_to_all | solution.py:21
  47.1 1.0 first.1
  48.1 2.6 %collective-permute-done.refs_1_ = bf16[256,128]{1,0:T(8,128)(2,1)S(1)} collective-permute-done((bf16[256,128]{1,0:T(8,128)(2,1)}, bf16[256,128]{1,0:T(8,128)(2,1)S(1)}, u32[]{:S(2)}, u32[]{:S(2)}) %collective-permute-start) | collective-permute-done | bytes 65568 | tf_op jit(solution)/shard_map/ppermute | solution.py:34
  50.7 8.1 %all_to_all.31.refs_0_ = f32[4,72,128]{2,1,0:T(8,128)S(1)} all-to-all(f32[4,72,128]{2,1,0:T(8,128)S(1)} %repeat.1), channel_id=1, replica_groups=mesh['zh'=4,'co'=2,'y'=4,'xh'=2,'xl'=2,'zl'=4] {'zl'}, dimensions={0} | all-to-all | bytes 294912 | tf_op jit(solution)/shard_map/all_to_all | solution.py:21
  58.8 0.4 round.1
  59.2 1.3 copy-done.1
  60.5 6.9 %all-to-all-start.3 = ((bf16[16,512,128]{2,1,0:T(8,128)(2,1)}), bf16[16,512,128]{2,1,0:T(8,128)(2,1)}, u32[]{:S(2)}, u32[]{:S(2)}) async-start(bf16[16,512,128]{2,1,0:T(8,128)(2,1)} %copy-done.1), calls=%async_computation.3 | async-start | bytes 4194304 | tf_op jit(solution)/shard_map/all_to_all | solution.py:21
  67.4 0.0 all-gather.3.cloned.1.call-start
  67.5 0.7 pad_maximum_fusion
  68.1 0.0 all-gather.3.cloned.1.call-update
  68.2 9.2 %collective-permute-start.1 = (bf16[256,128]{1,0:T(8,128)(2,1)S(1)}, bf16[256,128]{1,0:T(8,128)(2,1)S(1)}, u32[]{:S(2)}, u32[]{:S(2)}) collective-permute-start(bf16[256,128]{1,0:T(8,128)(2,1)S(1)} %get-tuple-element.22), channel_id=1, source_target_pairs={{0,0},{1,1},{2,2},{3,3},{4,4},{5,5},{6,6},{7,7},{8,64},{9,65},{10,... | collective-permute-start | bytes 196616 | tf_op jit(solution)/shard_map/ppermute | solution.py:34
  77.3 20.5 %collective-permute-done.1.refs_4_ = bf16[256,128]{1,0:T(8,128)(2,1)S(1)} collective-permute-done((bf16[256,128]{1,0:T(8,128)(2,1)S(1)}, bf16[256,128]{1,0:T(8,128)(2,1)S(1)}, u32[]{:S(2)}, u32[]{:S(2)}) %collective-permute-start.1) | collective-permute-done | bytes 65568 | tf_op jit(solution)/shard_map/ppermute | solution.py:34
  97.8 0.0 all-to-all-done.3.refs_0_
  97.8 2.2 %second.1 = (f32[64,128]{1,0:T(8,128)S(1)}, bf16[16,272,128]{2,1,0:T(8,128)(2,1)S(1)}) custom-call(bf16[16,512,128]{2,1,0:T(8,128)(2,1)} %all-to-all-done.3.refs_0_, bf16[128,8192]{1,0:T(8,128)(2,1)S(1)} %copy-done, f32[64,128]{1,0:T(8,128)S(1)} %get-tuple-element.28.refs_2_, f32[64,128]{1,0:T(8,128)S(1)} %get-tuple-element.21.refs_3_, ...), custom_call_target="tpu_custom_call" | custom-call | tf_op jit(solution)/shard_map/second/pallas_call | solution.py:49
  100.1 19.4 %all_to_all.32.refs_0_.refs_1_ = bf16[16,272,128]{2,1,0:T(8,128)(2,1)S(1)} all-to-all(bf16[16,272,128]{2,1,0:T(8,128)(2,1)S(1)} %get-tuple-element.23), channel_id=1, replica_groups=mesh['zh'=4,'co'=2,'y'=4,'xh'=2,'xl'=2,'zl'=4] {'y','xh','xl'}, dimensions={0} | all-to-all | bytes 2228224 | tf_op jit(solution)/shard_map/all_to_all | solution.py:21
  119.5 0.7 sums.1
  120.2 16.0 %all-to-all-start.5 = ((f32[32,2,128]{2,1,0:T(2,128)}), f32[32,2,128]{2,1,0:T(2,128)S(1)}, u32[]{:S(2)}, u32[]{:S(2)}) async-start(f32[32,2,128]{2,1,0:T(2,128)} %sums.1), calls=%async_computation.5 | async-start | bytes 65536 | tf_op jit(solution)/shard_map/all_to_all | solution.py:21
  136.2 0.0 all-gather.3.cloned.1.call-done
  136.3 1.2 copy-done.3
  137.5 2.7 %prepare.1 = (bf16[512,1024]{1,0:T(8,128)(2,1)S(1)}, bf16[512,1024]{1,0:T(8,128)(2,1)S(1)}, f32[8,2,64,128]{3,2,1,0:T(8,128)S(1)}) custom-call(bf16[16,512,128]{2,1,0:T(8,128)(2,1)} %all-to-all-done.3.refs_0_, bf16[16,272,128]{2,1,0:T(8,128)(2,1)S(1)} %all_to_all.32.refs_0_.refs_1_, f32[8,4,64,128]{3,2,1,0:T(8,128)S(1)} %bitcast.8), custom_call_target="tpu_custom_call" | custom-call | tf_op jit(solution)/shard_map/prepare/pallas_call | solution.py:49
  140.2 0.0 copy-start.4
  140.2 0.8 copy-done.4
  141.0 7.4 %all-to-all-done.5.refs_1_ = f32[32,2,128]{2,1,0:T(2,128)S(1)} async-done(((f32[32,2,128]{2,1,0:T(2,128)}), f32[32,2,128]{2,1,0:T(2,128)S(1)}, u32[]{:S(2)}, u32[]{:S(2)}) %all-to-all-start.5) | async-done | bytes 32800 | tf_op jit(solution)/shard_map/all_to_all | solution.py:21
  148.3 1.0 copy-done.5
  149.4 1.7 %counts.1 = (f32[64,128]{1,0:T(8,128)}, f32[128,1024]{1,0:T(8,128)}) custom-call(s32[1]{0:T(128)} %bitcast.refs_0_, f32[32,2,128]{2,1,0:T(2,128)S(1)} %all-to-all-done.5.refs_1_, f32[8,2,64,128]{3,2,1,0:T(8,128)S(1)} %copy-done.5, f32[64,128]{1,0:T(8,128)S(1)} %get-tuple-element.25.refs_3_, bf16[512,1024]{1,0:T(8,128)(2,1)S(1)} %get-tuple-element.26.refs_4_, ...), custom_call_target="tpu_custom_call" | custom-call | tf_op jit(solution)/shard_map/counts/pallas_call | solution.py:49
  (11 shorter events, 0.0 us)
Async XLA Ops:
  22.3 1.1 copy-start.2
  23.4 23.7 %copy-start = (bf16[128,8192]{1,0:T(8,128)(2,1)S(1)}, bf16[128,8192]{1,0:T(8,128)(2,1)}, u32[]{:S(2)}) copy-start(bf16[128,8192]{1,0:T(8,128)(2,1)} %refs_1_.3) | copy-start | bytes 6291460
  23.4 23.7 %copy-start.6 = (f32[64,128]{1,0:T(8,128)S(1)}, f32[64,128]{1,0:T(8,128)}, u32[]{:S(2)}) copy-start(f32[64,128]{1,0:T(8,128)} %get-tuple-element.17.refs_3_) | copy-start | bytes 98308
  23.4 23.7 %all-to-all-start.1 = ((bf16[16,304,128]{2,1,0:T(8,128)(2,1)}), bf16[16,304,128]{2,1,0:T(8,128)(2,1)S(1)}, u32[]{:S(2)}, u32[]{:S(2)}) async-start(bf16[16,304,128]{2,1,0:T(8,128)(2,1)} %copy-done.2), calls=%async_computation.1 | async-start | bytes 2490368 | tf_op jit(solution)/shard_map/all_to_all | solution.py:21
  30.3 20.4 %collective-permute-start = (bf16[256,128]{1,0:T(8,128)(2,1)}, bf16[256,128]{1,0:T(8,128)(2,1)S(1)}, u32[]{:S(2)}, u32[]{:S(2)}) collective-permute-start(bf16[256,128]{1,0:T(8,128)(2,1)} %get-tuple-element.19), channel_id=1, source_target_pairs={{0,0},{1,1},{2,2},{3,3},{4,4},{5,5},{6,6},{7,7},{8,64},{9,65},{10,... | collective-permute-start | bytes 196616 | tf_op jit(solution)/shard_map/ppermute | solution.py:34
  59.2 1.3 copy-start.1
  60.5 6.9 %copy-start.7 = (f32[2,64,128]{2,1,0:T(8,128)S(1)}, f32[2,64,128]{2,1,0:T(8,128)}, u32[]{:S(2)}) copy-start(f32[2,64,128]{2,1,0:T(8,128)} %param.5) | copy-start | bytes 196612
  60.5 37.3 %all-to-all-start.3 = ((bf16[16,512,128]{2,1,0:T(8,128)(2,1)}), bf16[16,512,128]{2,1,0:T(8,128)(2,1)}, u32[]{:S(2)}, u32[]{:S(2)}) async-start(bf16[16,512,128]{2,1,0:T(8,128)(2,1)} %copy-done.1), calls=%async_computation.3 | async-start | bytes 4194304 | tf_op jit(solution)/shard_map/all_to_all | solution.py:21
  67.4 68.8 %all-gather.3.cloned.1.call-start = ((), (), s32[]{:S(2)}) async-start(), calls=%async_computation.6 | async-start | bytes 1179648 | tf_op jit(solution)/shard_map/all_gather | solution.py:246
  68.2 29.7 %collective-permute-start.1 = (bf16[256,128]{1,0:T(8,128)(2,1)S(1)}, bf16[256,128]{1,0:T(8,128)(2,1)S(1)}, u32[]{:S(2)}, u32[]{:S(2)}) collective-permute-start(bf16[256,128]{1,0:T(8,128)(2,1)S(1)} %get-tuple-element.22), channel_id=1, source_target_pairs={{0,0},{1,1},{2,2},{3,3},{4,4},{5,5},{6,6},{7,7},{8,64},{9,65},{10,... | collective-permute-start | bytes 196616 | tf_op jit(solution)/shard_map/ppermute | solution.py:34
  120.2 28.1 %all-to-all-start.5 = ((f32[32,2,128]{2,1,0:T(2,128)}), f32[32,2,128]{2,1,0:T(2,128)S(1)}, u32[]{:S(2)}, u32[]{:S(2)}) async-start(f32[32,2,128]{2,1,0:T(2,128)} %sums.1), calls=%async_computation.5 | async-start | bytes 65536 | tf_op jit(solution)/shard_map/all_to_all | solution.py:21
  136.3 1.2 copy-start.3
  140.2 0.8 copy-start.4
  148.3 1.0 copy-start.5
Sparse Core Ops, SparseCore 0:
  71.0 51.7 all-gather.2
